TPU v7x, 512 devices: a whole 4x4x16 slice. The times are simulated.
512 devices in a mesh: ctx: 128 (over y_hi, z, x), grp: 4 (over y_lo, core).
Axes of the slice: x: 4, y: 4 (y_hi: 2, y_lo: 2; y = y_hi * 2 + y_lo), z: 16, core: 2. Of those that a mesh axis runs over, the one named last changes fastest.
Arguments:
- query_branch: bfloat16 [256, 16384], P('grp', 'ctx'), may hold values from -6 to 6
- key_branch: bfloat16 [256, 16384], P('grp', 'ctx'), may hold values from -6 to 6
- value_branch: bfloat16 [256, 16384], P('grp', 'ctx'), may hold values from -6 to 6
- query_taps: float32 [256, 3], P('grp'), may hold values from -3.5 to 3.5
- key_taps: float32 [256, 3], P('grp'), may hold values from -3.5 to 3.5
- value_taps: float32 [256, 3], P('grp'), may hold values from -3.5 to 3.5
- long_filter: float32 [16384], P('ctx'), may hold values from -4 to 4
- grad_out: bfloat16 [256, 16384], P('grp', 'ctx'), may hold values from -1.5 to 1.5
Outputs:
- grad_query: float32 [256, 16384], P('grp', 'ctx')
- grad_key: float32 [256, 16384], P('grp', 'ctx')
- grad_value: float32 [256, 16384], P('grp', 'ctx')
- grad_filter: float32 [16384], P('ctx')
All inputs are finite; a program needn't handle non-finite values.
Results may differ from a plain program's by a relative error of at most 0.00055.
Values may be sent and summed in bfloat16 or wider, within the bound.
A program may use at most 64 MiB of HBM per device.

v0:
```python
import math

import jax
import jax.numpy as jnp
from jax import lax
from jax.sharding import PartitionSpec as P

exact_prec = lax.Precision.HIGHEST


def shifted(value, axis, steps):
    count = lax.axis_size(axis)
    leading, last = (max(0, -steps), min(count, count - steps))
    return lax.ppermute(value, axis, [(source, source + steps) for source in range(leading, last)])


def phase_pair(product_ids, modulus):
    angles = (product_ids % modulus).astype(jnp.float32) * (2.0 * math.pi / modulus)
    return (jnp.cos(angles), jnp.sin(angles))


def short_conv(rim_rows, signal, weights):
    extended = jnp.concatenate([rim_rows.astype(jnp.float32), signal.astype(jnp.float32)], axis=1)
    count = signal.shape[1]
    return (
        weights[:, 0:1] * extended[:, 2:]
        + weights[:, 1:2] * extended[:, 1 : count + 1]
        + weights[:, 2:3] * extended[:, 0:count]
    )


def short_back(gradient, rim_rows, weights):
    extended = jnp.concatenate([gradient, rim_rows], axis=1)
    count = gradient.shape[1]
    return (
        weights[:, 0:1] * extended[:, 0:count]
        + weights[:, 1:2] * extended[:, 1 : count + 1]
        + weights[:, 2:3] * extended[:, 2:]
    )


def local(
    query_branch, key_branch, value_branch, query_taps, key_taps, value_taps, long_filter, grad_out
):
    seq_parts = lax.axis_size("ctx")
    my_index = lax.axis_index("ctx")
    channels, length_dev = query_branch.shape
    slices = length_dev // seq_parts
    full_len = 2 * seq_parts * length_dev
    item_count = 2 * channels + 1
    tail_rows = shifted(
        (
            query_branch[:, length_dev - 2 :],
            key_branch[:, length_dev - 2 :],
            value_branch[:, length_dev - 2 :],
        ),
        "ctx",
        1,
    )
    query_conv = short_conv(tail_rows[0], query_branch, query_taps)
    key_conv = short_conv(tail_rows[1], key_branch, key_taps)
    value_conv = short_conv(tail_rows[2], value_branch, value_taps)
    gated = key_conv * value_conv
    grad_long = grad_out.astype(jnp.float32) * query_conv
    part_ids = jnp.arange(seq_parts, dtype=jnp.int32)
    freq_order = jnp.concatenate(
        [part_ids, jnp.full((1,), seq_parts, jnp.int32), 2 * seq_parts - part_ids[1:]], axis=0
    )
    cos_parts, sin_parts = phase_pair(part_ids[:, None] * freq_order[None, :], 2 * seq_parts)
    local_pos = jnp.arange(slices, dtype=jnp.int32) * seq_parts + my_index
    cos_twist, sin_twist = phase_pair(local_pos[:, None] * freq_order[None, :], full_len)
    pos_ids = jnp.arange(length_dev, dtype=jnp.int32)
    cos_full, sin_full = phase_pair(pos_ids[:, None] * pos_ids[None, :], length_dev)
    cos_grid = cos_full.reshape(slices, seq_parts, length_dev)
    sin_grid = sin_full.reshape(slices, seq_parts, length_dev)
    signals = jnp.concatenate([gated, grad_long, long_filter[None, :]], axis=0).reshape(
        item_count, slices, seq_parts
    )
    pieces = lax.all_to_all(signals, "ctx", split_axis=2, concat_axis=2, tiled=True)
    real_part = jnp.einsum("irp,pk->irk", pieces, cos_parts, precision=exact_prec)
    imag_part = -jnp.einsum("irp,pk->irk", pieces, sin_parts, precision=exact_prec)
    first_re = real_part * cos_twist + imag_part * sin_twist
    first_im = imag_part * cos_twist - real_part * sin_twist
    mid_re, mid_im = (
        lax.all_to_all(
            first_re.reshape(item_count, slices, 2, seq_parts),
            "ctx",
            split_axis=3,
            concat_axis=3,
            tiled=True,
        ),
        lax.all_to_all(
            first_im.reshape(item_count, slices, 2, seq_parts),
            "ctx",
            split_axis=3,
            concat_axis=3,
            tiled=True,
        ),
    )
    out_re = jnp.einsum("irts,rsm->itm", mid_re, cos_grid, precision=exact_prec) + jnp.einsum(
        "irts,rsm->itm", mid_im, sin_grid, precision=exact_prec
    )
    out_im = jnp.einsum("irts,rsm->itm", mid_im, cos_grid, precision=exact_prec) - jnp.einsum(
        "irts,rsm->itm", mid_re, sin_grid, precision=exact_prec
    )
    gated_re = out_re[:channels]
    gated_im = out_im[:channels]
    grad_re = out_re[channels : 2 * channels]
    grad_im = out_im[channels : 2 * channels]
    filt_re = out_re[2 * channels :]
    filt_im = out_im[2 * channels :]
    prod_re = filt_re * gated_re - filt_im * gated_im
    prod_im = filt_re * gated_im + filt_im * gated_re
    back_re = grad_re * filt_re + grad_im * filt_im
    back_im = grad_im * filt_re - grad_re * filt_im
    cross_re = jnp.sum(grad_re * gated_re + grad_im * gated_im, axis=0, keepdims=True)
    cross_im = jnp.sum(grad_im * gated_re - grad_re * gated_im, axis=0, keepdims=True)
    cross_re, cross_im = lax.psum((cross_re, cross_im), "grp")
    stack_re = jnp.concatenate([prod_re, back_re, cross_re], axis=0)
    stack_im = jnp.concatenate([prod_im, back_im, cross_im], axis=0)
    stack_count = stack_re.shape[0]
    inv_re = jnp.einsum("itk,kb->itb", stack_re, cos_full, precision=exact_prec) - jnp.einsum(
        "itk,kb->itb", stack_im, sin_full, precision=exact_prec
    )
    inv_im = jnp.einsum("itk,kb->itb", stack_re, sin_full, precision=exact_prec) + jnp.einsum(
        "itk,kb->itb", stack_im, cos_full, precision=exact_prec
    )
    returned_re, returned_im = (
        lax.all_to_all(
            inv_re.reshape(stack_count, 2, slices, seq_parts),
            "ctx",
            split_axis=3,
            concat_axis=3,
            tiled=True,
        ),
        lax.all_to_all(
            inv_im.reshape(stack_count, 2, slices, seq_parts),
            "ctx",
            split_axis=3,
            concat_axis=3,
            tiled=True,
        ),
    )
    cos_back = cos_twist.reshape(slices, 2, seq_parts).transpose(1, 0, 2)
    sin_back = sin_twist.reshape(slices, 2, seq_parts).transpose(1, 0, 2)
    turn_re = returned_re * cos_back - returned_im * sin_back
    turn_im = returned_re * sin_back + returned_im * cos_back
    cos_inv = cos_parts.T.reshape(2, seq_parts, seq_parts)
    sin_inv = sin_parts.T.reshape(2, seq_parts, seq_parts)
    scale_all = 1.0 / (full_len * math.sqrt(seq_parts * length_dev))
    real_out = jnp.einsum("itrd,tdp->irp", turn_re, cos_inv, precision=exact_prec) - jnp.einsum(
        "itrd,tdp->irp", turn_im, sin_inv, precision=exact_prec
    )
    tokens = real_out * scale_all
    returned = lax.all_to_all(tokens, "ctx", split_axis=2, concat_axis=2, tiled=True).reshape(
        item_count, length_dev
    )
    long_out = returned[:channels]
    grad_gated = returned[channels : 2 * channels]
    grad_filter = returned[2 * channels]
    grad_qconv = grad_out.astype(jnp.float32) * long_out
    grad_kconv = grad_gated * value_conv
    grad_vconv = grad_gated * key_conv
    head_rows = shifted((grad_qconv[:, :2], grad_kconv[:, :2], grad_vconv[:, :2]), "ctx", -1)
    grad_query = short_back(grad_qconv, head_rows[0], query_taps)
    grad_key = short_back(grad_kconv, head_rows[1], key_taps)
    grad_value = short_back(grad_vconv, head_rows[2], value_taps)
    return (grad_query, grad_key, grad_value, grad_filter)


def solution(mesh):
    placed = (
        P("grp", "ctx"),
        P("grp", "ctx"),
        P("grp", "ctx"),
        P("grp", None),
        P("grp", None),
        P("grp", None),
        P("ctx"),
        P("grp", "ctx"),
    )
    return jax.shard_map(
        local,
        mesh=mesh,
        in_specs=placed,
        out_specs=(P("grp", "ctx"), P("grp", "ctx"), P("grp", "ctx"), P("ctx")),
        check_vma=False,
    )
```

profile of v0, /device:TPU:24, one launch (start us, length us, event | category | flops | bytes accessed | tf_op | source)
XLA Modules:
  0.0 228.3 jit_solution(5983336972876991886)
XLA Ops:
  1.4 3.5 %collective-permute-start.1 = (bf16[64,2]{1,0:T(8,128)(2,1)S(1)}, bf16[64,2]{1,0:T(8,128)(2,1)S(1)}, u32[]{:S(2)}, u32[]{:S(2)}) collective-permute-start(bf16[64,2]{1,0:T(8,128)(2,1)S(1)} %slice.138), channel_id=1, source_target_pairs={{0,4},{4,8},{8,12},{12,16},{16,20},{20,24},{24,28},{28,32},{32,36}... | collective-permute-start | bytes 776 | tf_op jit(solution)/shard_map/ppermute | solution.py:14
  5.1 3.5 %collective-permute-start = (bf16[64,2]{1,0:T(8,128)(2,1)S(1)}, bf16[64,2]{1,0:T(8,128)(2,1)S(1)}, u32[]{:S(2)}, u32[]{:S(2)}) collective-permute-start(bf16[64,2]{1,0:T(8,128)(2,1)S(1)} %slice.132), channel_id=1, source_target_pairs={{0,4},{4,8},{8,12},{12,16},{16,20},{20,24},{24,28},{28,32},{32,36}... | collective-permute-start | bytes 776 | tf_op jit(solution)/shard_map/ppermute | solution.py:14
  8.7 3.2 %collective-permute-start.2 = (bf16[64,2]{1,0:T(8,128)(2,1)S(1)}, bf16[64,2]{1,0:T(8,128)(2,1)S(1)}, u32[]{:S(2)}, u32[]{:S(2)}) collective-permute-start(bf16[64,2]{1,0:T(8,128)(2,1)S(1)} %slice.143), channel_id=1, source_target_pairs={{0,4},{4,8},{8,12},{12,16},{16,20},{20,24},{24,28},{28,32},{32,36}... | collective-permute-start | bytes 776 | tf_op jit(solution)/shard_map/ppermute | solution.py:14
  12.7 9.1 %collective-permute-done.2 = bf16[64,2]{1,0:T(8,128)(2,1)S(1)} collective-permute-done((bf16[64,2]{1,0:T(8,128)(2,1)S(1)}, bf16[64,2]{1,0:T(8,128)(2,1)S(1)}, u32[]{:S(2)}, u32[]{:S(2)}) %collective-permute-start.2) | collective-permute-done | bytes 288 | tf_op jit(solution)/shard_map/ppermute | solution.py:14
  23.6 15.6 %all-to-all-start = ((f32[129,1,128]{0,1,2:T(1,128)}), f32[129,1,128]{0,1,2:T(1,128)S(1)}, u32[]{:S(2)}, u32[]{:S(2)}) async-start(f32[129,1,128]{0,1,2:T(1,128)} %copy.36), calls=%async_computation | async-start | bytes 262144 | tf_op jit(solution)/shard_map/all_to_all | solution.py:79
  39.6 15.4 %all-to-all-done = f32[129,1,128]{0,1,2:T(1,128)S(1)} async-done(((f32[129,1,128]{0,1,2:T(1,128)}), f32[129,1,128]{0,1,2:T(1,128)S(1)}, u32[]{:S(2)}, u32[]{:S(2)}) %all-to-all-start) | async-done | bytes 66080 | tf_op jit(solution)/shard_map/all_to_all | solution.py:79
  56.7 0.8 copy.40
  57.5 9.0 %all-to-all-start.2 = ((f32[129,1,2,128]{0,2,1,3:T(2,128)}), f32[129,1,2,128]{0,2,1,3:T(2,128)S(1)}, u32[]{:S(2)}, u32[]{:S(2)}) async-start(f32[129,1,2,128]{0,2,1,3:T(2,128)} %copy.40), calls=%async_computation.2 | async-start | bytes 524288 | tf_op jit(solution)/shard_map/all_to_all | solution.py:92
  66.6 0.9 copy.38
  67.4 18.9 %all-to-all-done.2 = f32[129,1,2,128]{0,2,1,3:T(2,128)S(1)} async-done(((f32[129,1,2,128]{0,2,1,3:T(2,128)}), f32[129,1,2,128]{0,2,1,3:T(2,128)S(1)}, u32[]{:S(2)}, u32[]{:S(2)}) %all-to-all-start.2) | async-done | bytes 132128 | tf_op jit(solution)/shard_map/all_to_all | solution.py:92
  86.3 9.0 %all-to-all-start.1 = ((f32[129,1,2,128]{0,2,1,3:T(2,128)}), f32[129,1,2,128]{0,2,1,3:T(2,128)S(1)}, u32[]{:S(2)}, u32[]{:S(2)}) async-start(f32[129,1,2,128]{0,2,1,3:T(2,128)} %copy.38), calls=%async_computation.1 | async-start | bytes 524288 | tf_op jit(solution)/shard_map/all_to_all | solution.py:85
  95.9 18.2 %all-to-all-done.1 = f32[129,1,2,128]{0,2,1,3:T(2,128)S(1)} async-done(((f32[129,1,2,128]{0,2,1,3:T(2,128)}), f32[129,1,2,128]{0,2,1,3:T(2,128)S(1)}, u32[]{:S(2)}, u32[]{:S(2)}) %all-to-all-start.1) | async-done | bytes 132128 | tf_op jit(solution)/shard_map/all_to_all | solution.py:85
  115.9 5.7 %all-reduce = (f32[1,2,128]{2,0,1:T(1,128)S(1)}, f32[1,2,128]{2,0,1:T(1,128)S(1)}) all-reduce(f32[1,2,128]{2,0,1:T(1,128)S(1)} %bitcast.102, f32[1,2,128]{2,0,1:T(1,128)S(1)} %bitcast.103), channel_id=1, replica_groups=mesh['ctx'=128,'grp'=4] {'grp'}, use_global_device_ids=true, to_apply=%region_1.2 | all-reduce | flops 512 | bytes 4096 | tf_op jit(solution)/shard_map/psum | solution.py:118
  123.5 9.3 %all-to-all-start.3 = ((f32[129,2,1,128]{0,1,2,3:T(2,128)}), f32[129,2,1,128]{0,1,2,3:T(2,128)S(1)}, u32[]{:S(2)}, u32[]{:S(2)}) async-start(f32[129,2,1,128]{0,1,2,3:T(2,128)} %copy.42), calls=%async_computation.3 | async-start | bytes 524288 | tf_op jit(solution)/shard_map/all_to_all | solution.py:129
  134.7 21.1 %all-to-all-done.3 = f32[129,2,1,128]{0,1,2,3:T(2,128)S(1)} async-done(((f32[129,2,1,128]{0,1,2,3:T(2,128)}), f32[129,2,1,128]{0,1,2,3:T(2,128)S(1)}, u32[]{:S(2)}, u32[]{:S(2)}) %all-to-all-start.3) | async-done | bytes 132128 | tf_op jit(solution)/shard_map/all_to_all | solution.py:129
  155.8 9.0 %all-to-all-start.4 = ((f32[129,2,1,128]{0,1,2,3:T(2,128)}), f32[129,2,1,128]{0,1,2,3:T(2,128)S(1)}, u32[]{:S(2)}, u32[]{:S(2)}) async-start(f32[129,2,1,128]{0,1,2,3:T(2,128)} %copy.44), calls=%async_computation.4 | async-start | bytes 524288 | tf_op jit(solution)/shard_map/all_to_all | solution.py:136
  165.3 21.0 %all-to-all-done.4 = f32[129,2,1,128]{0,1,2,3:T(2,128)S(1)} async-done(((f32[129,2,1,128]{0,1,2,3:T(2,128)}), f32[129,2,1,128]{0,1,2,3:T(2,128)S(1)}, u32[]{:S(2)}, u32[]{:S(2)}) %all-to-all-start.4) | async-done | bytes 132128 | tf_op jit(solution)/shard_map/all_to_all | solution.py:136
  186.6 1.0 convolution_bitcast_fusion
  187.6 1.0 fusion.4
  188.7 24.0 %all_to_all.30 = f32[129,1,128]{0,1,2:T(1,128)S(1)} all-to-all(f32[129,1,128]{0,1,2:T(1,128)S(1)} %copy.48), channel_id=1, replica_groups=mesh['ctx'=128,'grp'=4] {'ctx'}, dimensions={2} | all-to-all | bytes 132096 | tf_op jit(solution)/shard_map/all_to_all | solution.py:155
  213.1 5.3 %collective-permute-start.3 = (f32[64,2]{1,0:T(8,128)S(1)}, f32[64,2]{1,0:T(8,128)S(1)}, u32[]{:S(2)}, u32[]{:S(2)}) collective-permute-start(f32[64,2]{1,0:T(8,128)S(1)} %bitcast.101), channel_id=1, source_target_pairs={{4,0},{8,4},{12,8},{16,12},{20,16},{24,20},{28,24},{32,28},{36,32}... | collective-permute-start | bytes 1544 | tf_op jit(solution)/shard_map/ppermute | solution.py:14
  218.3 3.1 %collective-permute-start.4 = (f32[64,2]{1,0:T(8,128)S(1)}, f32[64,2]{1,0:T(8,128)S(1)}, u32[]{:S(2)}, u32[]{:S(2)}) collective-permute-start(f32[64,2]{1,0:T(8,128)S(1)} %bitcast.100), channel_id=1, source_target_pairs={{4,0},{8,4},{12,8},{16,12},{20,16},{24,20},{28,24},{32,28},{36,32}... | collective-permute-start | bytes 1544 | tf_op jit(solution)/shard_map/ppermute | solution.py:14
  221.5 3.0 %collective-permute-start.5 = (f32[64,2]{1,0:T(8,128)S(1)}, f32[64,2]{1,0:T(8,128)S(1)}, u32[]{:S(2)}, u32[]{:S(2)}) collective-permute-start(f32[64,2]{1,0:T(8,128)S(1)} %bitcast.99), channel_id=1, source_target_pairs={{4,0},{8,4},{12,8},{16,12},{20,16},{24,20},{28,24},{32,28},{36,32}... | collective-permute-start | bytes 1544 | tf_op jit(solution)/shard_map/ppermute | solution.py:14
  224.5 1.5 slice_reduce_fusion
  (78 shorter events, 15.1 us)
Async XLA Ops:
  0.6 4.3 %copy-start.2 = (bf16[64,128]{1,0:T(8,128)(2,1)S(1)}, bf16[64,128]{1,0:T(8,128)(2,1)}, u32[]{:S(2)}) copy-start(bf16[64,128]{1,0:T(8,128)(2,1)} %param.9) | copy-start | bytes 49156
  1.4 7.2 %copy-start.1 = (bf16[64,128]{1,0:T(8,128)(2,1)S(1)}, bf16[64,128]{1,0:T(8,128)(2,1)}, u32[]{:S(2)}) copy-start(bf16[64,128]{1,0:T(8,128)(2,1)} %param.8) | copy-start | bytes 49156
  1.4 20.5 %collective-permute-start.1 = (bf16[64,2]{1,0:T(8,128)(2,1)S(1)}, bf16[64,2]{1,0:T(8,128)(2,1)S(1)}, u32[]{:S(2)}, u32[]{:S(2)}) collective-permute-start(bf16[64,2]{1,0:T(8,128)(2,1)S(1)} %slice.138), channel_id=1, source_target_pairs={{0,4},{4,8},{8,12},{12,16},{16,20},{20,24},{24,28},{28,32},{32,36}... | collective-permute-start | bytes 776 | tf_op jit(solution)/shard_map/ppermute | solution.py:14
  5.1 6.9 %copy-start.5 = (f32[64,3]{0,1:T(4,128)S(1)}, f32[64,3]{0,1:T(4,128)}, u32[]{:S(2)}) copy-start(f32[64,3]{0,1:T(4,128)} %param.13) | copy-start | bytes 2308
  5.1 6.9 %copy-start.6 = (f32[64,3]{0,1:T(4,128)S(1)}, f32[64,3]{0,1:T(4,128)}, u32[]{:S(2)}) copy-start(f32[64,3]{0,1:T(4,128)} %param.12) | copy-start | bytes 2308
  5.1 16.9 %collective-permute-start = (bf16[64,2]{1,0:T(8,128)(2,1)S(1)}, bf16[64,2]{1,0:T(8,128)(2,1)S(1)}, u32[]{:S(2)}, u32[]{:S(2)}) collective-permute-start(bf16[64,2]{1,0:T(8,128)(2,1)S(1)} %slice.132), channel_id=1, source_target_pairs={{0,4},{4,8},{8,12},{12,16},{16,20},{20,24},{24,28},{28,32},{32,36}... | collective-permute-start | bytes 776 | tf_op jit(solution)/shard_map/ppermute | solution.py:14
  8.7 3.3 %copy-start.4 = (f32[64,3]{0,1:T(4,128)S(1)}, f32[64,3]{0,1:T(4,128)}, u32[]{:S(2)}) copy-start(f32[64,3]{0,1:T(4,128)} %param.11) | copy-start | bytes 2308
  8.7 13.1 %collective-permute-start.2 = (bf16[64,2]{1,0:T(8,128)(2,1)S(1)}, bf16[64,2]{1,0:T(8,128)(2,1)S(1)}, u32[]{:S(2)}, u32[]{:S(2)}) collective-permute-start(bf16[64,2]{1,0:T(8,128)(2,1)S(1)} %slice.143), channel_id=1, source_target_pairs={{0,4},{4,8},{8,12},{12,16},{16,20},{20,24},{24,28},{28,32},{32,36}... | collective-permute-start | bytes 776 | tf_op jit(solution)/shard_map/ppermute | solution.py:14
  12.0 0.7 copy-start.3
  12.7 9.1 %copy-start = (bf16[64,128]{1,0:T(8,128)(2,1)S(1)}, bf16[64,128]{1,0:T(8,128)(2,1)}, u32[]{:S(2)}) copy-start(bf16[64,128]{1,0:T(8,128)(2,1)} %param.15) | copy-start | bytes 49156
  22.2 0.7 copy-start.7
  23.6 31.3 %all-to-all-start = ((f32[129,1,128]{0,1,2:T(1,128)}), f32[129,1,128]{0,1,2:T(1,128)S(1)}, u32[]{:S(2)}, u32[]{:S(2)}) async-start(f32[129,1,128]{0,1,2:T(1,128)} %copy.36), calls=%async_computation | async-start | bytes 262144 | tf_op jit(solution)/shard_map/all_to_all | solution.py:79
  57.5 28.8 %all-to-all-start.2 = ((f32[129,1,2,128]{0,2,1,3:T(2,128)}), f32[129,1,2,128]{0,2,1,3:T(2,128)S(1)}, u32[]{:S(2)}, u32[]{:S(2)}) async-start(f32[129,1,2,128]{0,2,1,3:T(2,128)} %copy.40), calls=%async_computation.2 | async-start | bytes 524288 | tf_op jit(solution)/shard_map/all_to_all | solution.py:92
  86.3 27.8 %all-to-all-start.1 = ((f32[129,1,2,128]{0,2,1,3:T(2,128)}), f32[129,1,2,128]{0,2,1,3:T(2,128)S(1)}, u32[]{:S(2)}, u32[]{:S(2)}) async-start(f32[129,1,2,128]{0,2,1,3:T(2,128)} %copy.38), calls=%async_computation.1 | async-start | bytes 524288 | tf_op jit(solution)/shard_map/all_to_all | solution.py:85
  123.5 32.3 %all-to-all-start.3 = ((f32[129,2,1,128]{0,1,2,3:T(2,128)}), f32[129,2,1,128]{0,1,2,3:T(2,128)S(1)}, u32[]{:S(2)}, u32[]{:S(2)}) async-start(f32[129,2,1,128]{0,1,2,3:T(2,128)} %copy.42), calls=%async_computation.3 | async-start | bytes 524288 | tf_op jit(solution)/shard_map/all_to_all | solution.py:129
  155.8 30.5 %all-to-all-start.4 = ((f32[129,2,1,128]{0,1,2,3:T(2,128)}), f32[129,2,1,128]{0,1,2,3:T(2,128)S(1)}, u32[]{:S(2)}, u32[]{:S(2)}) async-start(f32[129,2,1,128]{0,1,2,3:T(2,128)} %copy.44), calls=%async_computation.4 | async-start | bytes 524288 | tf_op jit(solution)/shard_map/all_to_all | solution.py:136
  213.1 13.0 %collective-permute-start.3 = (f32[64,2]{1,0:T(8,128)S(1)}, f32[64,2]{1,0:T(8,128)S(1)}, u32[]{:S(2)}, u32[]{:S(2)}) collective-permute-start(f32[64,2]{1,0:T(8,128)S(1)} %bitcast.101), channel_id=1, source_target_pairs={{4,0},{8,4},{12,8},{16,12},{20,16},{24,20},{28,24},{32,28},{36,32}... | collective-permute-start | bytes 1544 | tf_op jit(solution)/shard_map/ppermute | solution.py:14
  218.3 8.4 %collective-permute-start.4 = (f32[64,2]{1,0:T(8,128)S(1)}, f32[64,2]{1,0:T(8,128)S(1)}, u32[]{:S(2)}, u32[]{:S(2)}) collective-permute-start(f32[64,2]{1,0:T(8,128)S(1)} %bitcast.100), channel_id=1, source_target_pairs={{4,0},{8,4},{12,8},{16,12},{20,16},{24,20},{28,24},{32,28},{36,32}... | collective-permute-start | bytes 1544 | tf_op jit(solution)/shard_map/ppermute | solution.py:14
  221.5 6.1 %collective-permute-start.5 = (f32[64,2]{1,0:T(8,128)S(1)}, f32[64,2]{1,0:T(8,128)S(1)}, u32[]{:S(2)}, u32[]{:S(2)}) collective-permute-start(f32[64,2]{1,0:T(8,128)S(1)} %bitcast.99), channel_id=1, source_target_pairs={{4,0},{8,4},{12,8},{16,12},{20,16},{24,20},{28,24},{32,28},{36,32}... | collective-permute-start | bytes 1544 | tf_op jit(solution)/shard_map/ppermute | solution.py:14
where the time goes:
time: 229 us; the launch traced here: 228 us
  waiting for transfers between devices  104 us (45%)
  starting transfers between devices  73.6 us (32%)
  blocking collectives  29.7 us (13%)
  local copies, waits for them, and re-layouts  9.28 us (4%)
  matrix products  7.59 us (3%)
  other arithmetic  3.4 us (1%)
    all_to_all x1, blocking collectives, local(): lax.all_to_all(tokens, 'ctx', split_axis=2, concat_axis=2, tiled=True)  24 us
    ppermute x6, starting transfers between devices, shifted(): lax.ppermute(value, axis, [(source, source + steps) for source in range(l...  21.7 us
    all_to_all x1, waiting for transfers between devices, local(): lax.all_to_all(inv_re.reshape(stack_count, 2, slices, seq_parts), 'ctx',...  21.1 us
    all_to_all x1, waiting for transfers between devices, local(): lax.all_to_all(inv_im.reshape(stack_count, 2, slices, seq_parts), 'ctx',...  21 us
    all_to_all x1, waiting for transfers between devices, local(): lax.all_to_all(first_im.reshape(item_count, slices, 2, seq_parts), 'ctx',...  18.9 us
    all_to_all x1, waiting for transfers between devices, local(): lax.all_to_all(first_re.reshape(item_count, slices, 2, seq_parts), 'ctx',...  18.2 us
    all_to_all x1, starting transfers between devices, local(): lax.all_to_all(signals, 'ctx', split_axis=2, concat_axis=2, tiled=True)  15.6 us
    all_to_all x1, waiting for transfers between devices, local(): lax.all_to_all(signals, 'ctx', split_axis=2, concat_axis=2, tiled=True)  15.4 us
  transfers between devices with their start and end apart: 11, of which 6 were waited for; matrix products, arithmetic and copies ran while one was open for 3% of the time, Pallas kernels for 0%

commit v1 on v0

v1 whole, which is shorter than its diff:
```python
import functools
import math

import jax
import jax.numpy as jnp
import ml_dtypes
import numpy as np
from jax import lax
from jax.experimental import pallas as pl
from jax.experimental.pallas import tpu as pltpu
from jax.sharding import PartitionSpec as P

NY, NZ, NX, NG = 2, 16, 4, 4
NP = NY * NX
NI = NP // 2
BLK = 128
NB = NY * NZ * NX
FULL = 2 * BLK * NB
MESH = pl.DeviceIdType.MESH
Z_STEPS = (8, 7, 9, 6, 10, 5, 11, 4, 12, 3, 13, 2, 14, 1, 15)
F32, BF16 = jnp.float32, jnp.bfloat16


def split_np(matrix):
    high = matrix.astype(np.float32).astype(ml_dtypes.bfloat16)
    low = (matrix - high.astype(np.float64)).astype(np.float32).astype(ml_dtypes.bfloat16)
    return np.stack([high, low])


@functools.lru_cache(maxsize=None)
def tables():
    half = np.arange(NB) + 0.5
    blocks = np.arange(NB)
    pos = np.arange(BLK)
    outer = 2.0 * np.pi * half[:, None] * blocks[None, :] / (2 * NB)
    fwd_outer = np.concatenate([np.cos(outer), -np.sin(outer)], axis=0)
    twist = 2.0 * np.pi * half[:, None] * pos[None, :] / FULL
    twists = np.stack([np.cos(twist), np.sin(twist)]).astype(np.float32)
    inner = 2.0 * np.pi * ((pos[:, None] * pos[None, :]) % BLK) / BLK
    cos, sin = np.cos(inner), np.sin(inner)
    fwd_inner = np.block([[cos, -sin], [sin, cos]])
    scale = 2.0 / (FULL * math.sqrt(BLK * NB))
    inv_outer = scale * np.concatenate([np.cos(outer).T, -np.sin(outer).T], axis=1)
    return (
        split_np(fwd_outer),
        twists,
        split_np(fwd_inner),
        split_np(fwd_inner.T.copy()),
        split_np(inv_outer),
    )


def split(value):
    high = value.astype(BF16)
    return high, (value - high.astype(F32)).astype(BF16)


def dot(left, right):
    return jnp.dot(left, right, preferred_element_type=F32)


def left_table(table, value):
    high, low = split(value)
    return dot(table[0], high) + (dot(table[0], low) + dot(table[1], high))


def right_table(value, table):
    high, low = split(value)
    return dot(high, table[0]) + (dot(low, table[0]) + dot(high, table[1]))


def earlier(value, steps):
    lane = lax.broadcasted_iota(jnp.int32, value.shape, 1)
    row = lax.broadcasted_iota(jnp.int32, value.shape, 0)
    turned = pltpu.roll(value, steps, 1)
    above = jnp.where(row == 0, 0.0, pltpu.roll(turned, 1, 0))
    return jnp.where(lane < steps, above, turned)


def later(value, steps):
    lane = lax.broadcasted_iota(jnp.int32, value.shape, 1)
    row = lax.broadcasted_iota(jnp.int32, value.shape, 0)
    turned = pltpu.roll(value, BLK - steps, 1)
    below = jnp.where(row == NB - 1, 0.0, pltpu.roll(turned, NB - 1, 0))
    return jnp.where(lane >= BLK - steps, below, turned)


def kernel(
    q_ref, k_ref, v_ref, g_ref, tq_ref, tk_ref, tv_ref, filt_ref,
    fo_hbm, tw_hbm, fi_hbm, ii_hbm, io_hbm,
    oq_ref, ok_ref, ov_ref, of_ref,
    fo, tw, fi, ii, io,
    stage, s1, r1, r1f, s2, r2, s2f, r2f, tok, res, s3, r3, s4, r4, s5, r5,
    const_sem, z_send, z_recv, zf_send, zf_recv, p_send, p_recv, pf_send, pf_recv,
    b_send, b_recv, c_send, c_recv, g_send, g_recv,
):
    me = lax.axis_index("ctx")
    grp = lax.axis_index("grp")
    y, z, x = me // (NZ * NX), (me // NX) % NZ, me % NX
    p = y * NX + x
    pair, role = p // 2, p % 2

    def z_peer(step):
        other = (z + step) % NZ
        return other, {"ctx": (y * NZ + other) * NX + x}

    def p_peer(step):
        other = (p + step) % NP
        return other, {"ctx": ((other // NX) * NZ + z) * NX + other % NX}

    def g_peer(step):
        return {"grp": (grp + step) % NG}

    barrier = pltpu.get_barrier_semaphore()
    for step in Z_STEPS:
        pl.semaphore_signal(barrier, inc=1, device_id=z_peer(step)[1], device_id_type=MESH)
    for step in range(1, NP):
        pl.semaphore_signal(barrier, inc=1, device_id=p_peer(step)[1], device_id_type=MESH)
    for step in range(1, NG):
        pl.semaphore_signal(barrier, inc=1, device_id=g_peer(step), device_id_type=MESH)

    loads = [
        pltpu.make_async_copy(src, dst, const_sem.at[n])
        for n, (src, dst) in enumerate(
            ((fo_hbm, fo), (tw_hbm, tw), (fi_hbm, fi), (ii_hbm, ii), (io_hbm, io))
        )
    ]
    for load in loads:
        load.start()

    sends = []

    def send(src, dst, send_sem, recv_sem, target):
        copy = pltpu.make_async_remote_copy(
            src_ref=src, dst_ref=dst, send_sem=send_sem, recv_sem=recv_sem,
            device_id=target, device_id_type=MESH,
        )
        copy.start()
        sends.append(copy)

    def arrived(ref, sem):
        pltpu.make_async_copy(ref, ref, sem).wait()

    channels = q_ref.shape[0]
    for n, ref in enumerate((q_ref, k_ref, v_ref, g_ref)):
        stage[n * channels : (n + 1) * channels, :] = ref[...].astype(F32)
    for other in range(NZ):
        s1[other] = stage[pl.ds(other, 16, stride=NZ), :].astype(BF16)
    pl.semaphore_wait(barrier, len(Z_STEPS) + NP - 1 + NG - 1)

    for n, step in enumerate(Z_STEPS):
        other, target = z_peer(step)
        send(s1.at[other], r1.at[z], z_send.at[n], z_recv, target)
    for n, step in enumerate(Z_STEPS):
        other, target = z_peer(step)
        send(filt_ref, r1f.at[z], zf_send.at[n], zf_recv, target)
    r1[z] = s1[z]
    r1f[z] = filt_ref[...]
    arrived(r1.at[pl.ds(0, NZ - 1)], z_recv)

    stage[...] = r1[...].astype(F32).reshape(NZ * 16, BLK)
    for i in range(NI):
        for n in range(4):
            s2[i, n] = stage[pl.ds(n * NI + i, NZ, stride=16), :].astype(BF16)
    for n, step in enumerate(range(1, NP)):
        other, target = p_peer(step)
        send(s2.at[other // 2], r2.at[p], p_send.at[n], p_recv, target)
    arrived(r1f.at[pl.ds(0, NZ - 1)], zf_recv)
    s2f[...] = r1f[...].reshape(NZ, BLK)
    for n, step in enumerate(range(1, NP)):
        other, target = p_peer(step)
        send(s2f, r2f.at[p], pf_send.at[n], pf_recv, target)
    r2[p] = s2[pair]
    r2f[p] = s2f[...]
    arrived(r2.at[pl.ds(0, NP - 1)], p_recv)

    def rows_of(other):
        return pl.ds((other // NX) * NZ * NX + other % NX, NZ, stride=NX)

    for other in range(NP):
        for n in range(4):
            tok[n, rows_of(other), :] = r2[other, n].astype(F32)
    arrived(r2f.at[pl.ds(0, NP - 1)], pf_recv)
    for other in range(NP):
        tok[4, rows_of(other), :] = r2f[other]

    channel = z + NZ * pair
    taps = [[ref[channel, j] for j in range(3)] for ref in (tq_ref, tk_ref, tv_ref)]

    def conv(value, weights):
        return weights[0] * value + weights[1] * earlier(value, 1) + weights[2] * earlier(value, 2)

    grad_out = tok[3]
    key_conv = conv(tok[1], taps[1])
    value_conv = conv(tok[2], taps[2])
    gated = key_conv * value_conv
    grad_long = grad_out * conv(tok[0], taps[0])

    for load in loads:
        load.wait()
    signals = jnp.concatenate([gated, grad_long, tok[4]], axis=1)
    outer = left_table(fo, signals)
    cos, sin = tw[0], tw[1]
    turned = []
    for n in range(3):
        re = outer[:NB, n * BLK : (n + 1) * BLK]
        im = outer[NB:, n * BLK : (n + 1) * BLK]
        turned.append(jnp.concatenate([re * cos + im * sin, im * cos - re * sin], axis=1))
    spectra = right_table(jnp.concatenate(turned, axis=0), fi)
    gated_re, gated_im = spectra[:NB, :BLK], spectra[:NB, BLK:]
    grad_re, grad_im = spectra[NB : 2 * NB, :BLK], spectra[NB : 2 * NB, BLK:]
    filt_re, filt_im = spectra[2 * NB :, :BLK], spectra[2 * NB :, BLK:]

    first = role == 0
    left_re = jnp.where(first, gated_re, grad_re)
    left_im = jnp.where(first, gated_im, grad_im)
    turn_im = jnp.where(first, filt_im, -filt_im)
    main = jnp.concatenate(
        [left_re * filt_re - left_im * turn_im, left_re * turn_im + left_im * filt_re], axis=1
    )
    cross = jnp.concatenate(
        [grad_re * gated_re + grad_im * gated_im, grad_im * gated_re - grad_re * gated_im], axis=1
    )
    inner = right_table(jnp.concatenate([main, cross], axis=0), ii)
    backs = []
    for n in range(2):
        re = inner[n * NB : (n + 1) * NB, :BLK]
        im = inner[n * NB : (n + 1) * NB, BLK:]
        backs.append(jnp.concatenate([re * cos - im * sin, im * cos + re * sin], axis=0))
    tokens = left_table(io, jnp.concatenate(backs, axis=1))
    main_tok, cross_tok = tokens[:, :BLK], tokens[:, BLK:]

    def back(value, weights):
        return weights[0] * value + weights[1] * later(value, 1) + weights[2] * later(value, 2)

    def chosen(mine, other):
        return [jnp.where(first, a, b) for a, b in zip(mine, other)]

    res[0] = back(
        main_tok * jnp.where(first, grad_out, value_conv), chosen(taps[0], taps[1])
    )
    res[1] = jnp.where(first, cross_tok, back(main_tok * key_conv, taps[2]))

    for other in range(NP):
        for n in range(2):
            s3[other, n] = res[n, rows_of(other), :]
    for n, step in enumerate(range(1, NP)):
        other, target = p_peer(step)
        send(s3.at[other], r3.at[p], b_send.at[n], b_recv, target)
    r3[p] = s3[p]
    arrived(r3.at[pl.ds(0, NP - 1)], b_recv)

    for i in range(NI):
        s4[pl.ds(i, NZ, stride=16), :] = r3[2 * i, 0]
        s4[pl.ds(NI + i, NZ, stride=16), :] = r3[2 * i + 1, 0]
        s4[pl.ds(2 * NI + i, NZ, stride=16), :] = r3[2 * i + 1, 1]
    s4[pl.ds(12, NZ, stride=16), :] = (r3[0, 1] + r3[2, 1]) + (r3[4, 1] + r3[6, 1])
    for other in range(3):
        s4[pl.ds(13 + other, NZ, stride=16), :] = jnp.zeros((NZ, BLK), F32)
    my_rows = pl.ds(pl.multiple_of(z * 16, 16), 16)
    for n, step in enumerate(Z_STEPS):
        other, target = z_peer(step)
        rows = pl.ds(pl.multiple_of(other * 16, 16), 16)
        send(s4.at[rows], r4.at[my_rows], c_send.at[n], c_recv, target)
    r4[my_rows, :] = s4[my_rows, :]
    arrived(r4.at[pl.ds(0, (NZ - 1) * 16)], c_recv)

    total = jnp.sum(r4[pl.ds(12, NZ, stride=16), :], axis=0, keepdims=True)
    s5[...] = total
    for n, step in enumerate(range(1, NG)):
        send(s5, r5.at[grp], g_send.at[n], g_recv, g_peer(step))
    r5[grp] = total
    for n, ref in enumerate((oq_ref, ok_ref, ov_ref)):
        for i in range(NI):
            ref[i * NZ : (i + 1) * NZ, :] = r4[pl.ds(n * NI + i, NZ, stride=16), :]
    arrived(r5.at[pl.ds(0, NG - 1)], g_recv)
    of_ref[...] = (r5[0] + r5[1]) + (r5[2] + r5[3])
    for copy in sends:
        copy.wait_send()


def local(query_branch, key_branch, value_branch, query_taps, key_taps, value_taps, long_filter, grad_out):
    channels, count = query_branch.shape
    vmem = pl.BlockSpec(memory_space=pltpu.VMEM)
    smem = pl.BlockSpec(memory_space=pltpu.SMEM)
    hbm = pl.BlockSpec(memory_space=pl.ANY)
    consts = [jnp.asarray(table) for table in tables()]
    token_out = jax.ShapeDtypeStruct((channels, count), F32)
    sems = pltpu.SemaphoreType.DMA
    outs = pl.pallas_call(
        kernel,
        out_shape=(token_out, token_out, token_out, jax.ShapeDtypeStruct((1, count), F32)),
        in_specs=[vmem] * 4 + [smem] * 3 + [vmem] + [hbm] * 5,
        out_specs=(vmem,) * 4,
        scratch_shapes=[pltpu.VMEM(c.shape, c.dtype) for c in consts]
        + [
            pltpu.VMEM((4 * channels, BLK), F32),
            pltpu.VMEM((NZ, 16, BLK), BF16),
            pltpu.VMEM((NZ, 16, BLK), BF16),
            pltpu.VMEM((NZ, 1, BLK), F32),
            pltpu.VMEM((NI, 4, NZ, BLK), BF16),
            pltpu.VMEM((NP, 4, NZ, BLK), BF16),
            pltpu.VMEM((NZ, BLK), F32),
            pltpu.VMEM((NP, NZ, BLK), F32),
            pltpu.VMEM((5, NB, BLK), F32),
            pltpu.VMEM((2, NB, BLK), F32),
            pltpu.VMEM((NP, 2, NZ, BLK), F32),
            pltpu.VMEM((NP, 2, NZ, BLK), F32),
            pltpu.VMEM((NZ * 16, BLK), F32),
            pltpu.VMEM((NZ * 16, BLK), F32),
            pltpu.VMEM((1, BLK), F32),
            pltpu.VMEM((NG, 1, BLK), F32),
            sems((5,)),
            sems((NZ - 1,)), sems(()), sems((NZ - 1,)), sems(()),
            sems((NP - 1,)), sems(()), sems((NP - 1,)), sems(()),
            sems((NP - 1,)), sems(()),
            sems((NZ - 1,)), sems(()),
            sems((NG - 1,)), sems(()),
        ],
        compiler_params=pltpu.CompilerParams(
            collective_id=0, has_side_effects=True, vmem_limit_bytes=32 * 1024 * 1024
        ),
    )(
        query_branch, key_branch, value_branch, grad_out,
        query_taps, key_taps, value_taps, long_filter.reshape(1, count), *consts,
    )
    return outs[0], outs[1], outs[2], outs[3].reshape(count)


def solution(mesh):
    tokens = P("grp", "ctx")
    taps = P("grp", None)
    return jax.shard_map(
        local,
        mesh=mesh,
        in_specs=(tokens, tokens, tokens, taps, taps, taps, P("ctx"), tokens),
        out_specs=(tokens, tokens, tokens, P("ctx")),
        check_vma=False,
    )
```

time: 229 us -> 60.5 us (0.26)
  the two profiles are of different devices: /device:TPU:24 before, /device:TPU:1 now
where the time goes in v1:
time: 60.5 us; the launch traced here: 60.1 us
  Pallas kernels  50.3 us (83%)
  local copies, waits for them, and re-layouts  9.14 us (15%)
  between operations  0.69 us (1%)
    pallas_call x1, Pallas kernels, local(): pl.pallas_call(kernel, out_shape=(token_out, token_out, token_out, jax.Sh...  50.3 us
    unnamed x31, local copies, waits for them, and re-layouts  9.14 us

profile of v1, /device:TPU:1, one launch (start us, length us, event | category | flops | bytes accessed | tf_op | source)
XLA Modules:
  0.0 60.1 jit_solution(5925949482723717876)
XLA Ops:
  0.6 0.0 copy-start.10
  0.6 0.8 %copy.17.tq_ref = f32[64,3]{1,0:T(8,128)S(1)} copy(f32[64,3]{0,1:T(4,128)} %param.16) | data formatting | bytes 1536 | tf_op args[3]
  1.4 0.0 copy-done.10
  1.4 0.0 copy-start.11
  1.4 0.0 copy-start.7
  1.4 0.0 copy-start.8
  1.5 0.1 copy.18.tk_ref
  1.6 0.6 copy-done.11
  2.1 0.1 copy.19.tv_ref
  2.2 0.0 copy-done.7
  2.2 0.0 copy-done.8
  2.2 0.6 %copy-done.5 = bf16[64,128]{1,0:T(8,128)(2,1)S(1)} copy-done((bf16[64,128]{1,0:T(8,128)(2,1)S(1)}, bf16[64,128]{1,0:T(8,128)(2,1)}, u32[]{:S(2)}) %copy-start.5) | copy-done | bytes 16408
  2.8 0.0 copy-done.6
  2.8 0.0 copy-done.9
  2.8 0.9 %copy-done = bf16[2,256,256]{2,1,0:T(8,128)(2,1)S(1)} copy-done((bf16[2,256,256]{2,1,0:T(8,128)(2,1)S(1)}, bf16[2,256,256]{2,1,0:T(8,128)(2,1)}, u32[]{:S(2)}) %copy-start) | copy-done | bytes 262168
  3.8 0.9 %copy-done.1 = bf16[2,256,256]{2,1,0:T(8,128)(2,1)S(1)} copy-done((bf16[2,256,256]{2,1,0:T(8,128)(2,1)S(1)}, bf16[2,256,256]{2,1,0:T(8,128)(2,1)}, u32[]{:S(2)}) %copy-start.1) | copy-done | bytes 262168
  4.7 0.9 %copy-done.2 = bf16[2,128,256]{2,1,0:T(8,128)(2,1)S(1)} copy-done((bf16[2,128,256]{2,1,0:T(8,128)(2,1)S(1)}, bf16[2,128,256]{2,1,0:T(8,128)(2,1)}, u32[]{:S(2)}) %copy-start.2) | copy-done | bytes 131096
  5.7 0.9 %copy-done.3 = f32[2,128,128]{2,1,0:T(8,128)S(1)} copy-done((f32[2,128,128]{2,1,0:T(8,128)S(1)}, f32[2,128,128]{2,1,0:T(8,128)}, u32[]{:S(2)}) %copy-start.3) | copy-done | bytes 131096
  6.6 0.9 %copy-done.4 = bf16[2,256,128]{2,1,0:T(8,128)(2,1)S(1)} copy-done((bf16[2,256,128]{2,1,0:T(8,128)(2,1)S(1)}, bf16[2,256,128]{2,1,0:T(8,128)(2,1)}, u32[]{:S(2)}) %copy-start.4) | copy-done | bytes 131096
  7.5 50.3 %shard_map.156 = (f32[64,128]{1,0:T(8,128)S(1)}, f32[64,128]{1,0:T(8,128)S(1)}, f32[64,128]{1,0:T(8,128)S(1)}, f32[1,128]{1,0:T(1,128)S(1)}) custom-call(bf16[64,128]{1,0:T(8,128)(2,1)S(1)} %copy-done.5, bf16[64,128]{1,0:T(8,128)(2,1)S(1)} %copy-done.6, bf16[64,128]{1,0:T(8,128)(2,1)S(1)} %copy-done.7, bf16[64,128]{1,0:T(8,128)(2,1)S(1)} %copy-done.8, ...), custom_call_target="tpu_custom_call" | custom-call | tf_op jit(solution)/shard_map/pallas_call | solution.py:290
  57.8 0.6 %copy.24 = f32[64,128]{1,0:T(8,128)} copy(f32[64,128]{1,0:T(8,128)S(1)} %get-tuple-element.16) | data formatting | bytes 65536
  58.4 0.6 %copy.25 = f32[64,128]{1,0:T(8,128)} copy(f32[64,128]{1,0:T(8,128)S(1)} %get-tuple-element.17) | data formatting | bytes 65536
  59.0 0.6 %copy.26 = f32[64,128]{1,0:T(8,128)} copy(f32[64,128]{1,0:T(8,128)S(1)} %get-tuple-element.18) | data formatting | bytes 65536
  59.6 0.5 copy.27
  (8 shorter events, 0.0 us)
Async XLA Ops:
  0.6 0.8 %copy-start.10 = (f32[64,3]{0,1:T(4,128)S(1)}, f32[64,3]{0,1:T(4,128)}, u32[]{:S(2)}) copy-start(f32[64,3]{0,1:T(4,128)} %param.17) | copy-start | bytes 2308
  1.4 0.7 %copy-start.11 = (f32[64,3]{0,1:T(4,128)S(1)}, f32[64,3]{0,1:T(4,128)}, u32[]{:S(2)}) copy-start(f32[64,3]{0,1:T(4,128)} %param.18) | copy-start | bytes 2308
  1.4 0.8 %copy-start.7 = (bf16[64,128]{1,0:T(8,128)(2,1)S(1)}, bf16[64,128]{1,0:T(8,128)(2,1)}, u32[]{:S(2)}) copy-start(bf16[64,128]{1,0:T(8,128)(2,1)} %v_ref.1) | copy-start | bytes 49156
  1.4 0.8 %copy-start.8 = (bf16[64,128]{1,0:T(8,128)(2,1)S(1)}, bf16[64,128]{1,0:T(8,128)(2,1)}, u32[]{:S(2)}) copy-start(bf16[64,128]{1,0:T(8,128)(2,1)} %g_ref.1) | copy-start | bytes 49156
  2.1 0.7 %copy-start.5 = (bf16[64,128]{1,0:T(8,128)(2,1)S(1)}, bf16[64,128]{1,0:T(8,128)(2,1)}, u32[]{:S(2)}) copy-start(bf16[64,128]{1,0:T(8,128)(2,1)} %q_ref.1) | copy-start | bytes 49156
  2.1 0.7 %copy-start.6 = (bf16[64,128]{1,0:T(8,128)(2,1)S(1)}, bf16[64,128]{1,0:T(8,128)(2,1)}, u32[]{:S(2)}) copy-start(bf16[64,128]{1,0:T(8,128)(2,1)} %k_ref.1) | copy-start | bytes 49156
  2.1 0.7 %copy-start.9 = (f32[128]{0:T(128)S(1)}, f32[128]{0:T(128)}, u32[]{:S(2)}) copy-start(f32[128]{0:T(128)} %param.19) | copy-start | bytes 1540
  2.8 1.0 %copy-start = (bf16[2,256,256]{2,1,0:T(8,128)(2,1)S(1)}, bf16[2,256,256]{2,1,0:T(8,128)(2,1)}, u32[]{:S(2)}) copy-start(bf16[2,256,256]{2,1,0:T(8,128)(2,1)} %constant.13.clone.ii_hbm) | copy-start | bytes 786436
  3.8 0.9 %copy-start.1 = (bf16[2,256,256]{2,1,0:T(8,128)(2,1)S(1)}, bf16[2,256,256]{2,1,0:T(8,128)(2,1)}, u32[]{:S(2)}) copy-start(bf16[2,256,256]{2,1,0:T(8,128)(2,1)} %constant.12.clone.fi_hbm) | copy-start | bytes 786436
  4.7 0.9 %copy-start.2 = (bf16[2,128,256]{2,1,0:T(8,128)(2,1)S(1)}, bf16[2,128,256]{2,1,0:T(8,128)(2,1)}, u32[]{:S(2)}) copy-start(bf16[2,128,256]{2,1,0:T(8,128)(2,1)} %constant.14.clone.io_hbm) | copy-start | bytes 393220
  5.6 0.9 %copy-start.3 = (f32[2,128,128]{2,1,0:T(8,128)S(1)}, f32[2,128,128]{2,1,0:T(8,128)}, u32[]{:S(2)}) copy-start(f32[2,128,128]{2,1,0:T(8,128)} %constant.11.clone.tw_hbm) | copy-start | bytes 393220
  6.6 0.9 %copy-start.4 = (bf16[2,256,128]{2,1,0:T(8,128)(2,1)S(1)}, bf16[2,256,128]{2,1,0:T(8,128)(2,1)}, u32[]{:S(2)}) copy-start(bf16[2,256,128]{2,1,0:T(8,128)(2,1)} %constant.10.clone.fo_hbm) | copy-start | bytes 393220

commit v2 on v1

--- a/solution.py
+++ b/solution.py
@@ -86,12 +86,13 @@
 
 
 def kernel(
-    q_ref, k_ref, v_ref, g_ref, tq_ref, tk_ref, tv_ref, filt_ref,
+    q_hbm, k_hbm, v_hbm, g_hbm, filt_hbm, tq_hbm, tk_hbm, tv_hbm,
     fo_hbm, tw_hbm, fi_hbm, ii_hbm, io_hbm,
-    oq_ref, ok_ref, ov_ref, of_ref,
+    r4, of_ref,
+    q_ref, k_ref, v_ref, g_ref, filt_ref, tq_ref, tk_ref, tv_ref,
     fo, tw, fi, ii, io,
-    stage, s1, r1, r1f, s2, r2, s2f, r2f, tok, res, s3, r3, s4, r4, s5, r5,
-    const_sem, z_send, z_recv, zf_send, zf_recv, p_send, p_recv, pf_send, pf_recv,
+    stage, s1, r1, r1f, s2, r2, s2f, r2f, tok, res, s3, r3, s4, s5, r5,
+    load_sem, z_send, z_recv, zf_send, zf_recv, p_send, p_recv, pf_send, pf_recv,
     b_send, b_recv, c_send, c_recv, g_send, g_recv,
 ):
     me = lax.axis_index("ctx")
@@ -111,6 +112,18 @@
     def g_peer(step):
         return {"grp": (grp + step) % NG}
 
+    loads = [
+        pltpu.make_async_copy(src, dst, load_sem.at[n])
+        for n, (src, dst) in enumerate(
+            (
+                (q_hbm, q_ref), (k_hbm, k_ref), (v_hbm, v_ref), (g_hbm, g_ref), (filt_hbm, filt_ref),
+                (tq_hbm, tq_ref), (tk_hbm, tk_ref), (tv_hbm, tv_ref),
+                (fo_hbm, fo), (tw_hbm, tw), (fi_hbm, fi), (ii_hbm, ii), (io_hbm, io),
+            )
+        )
+    ]
+    for load in loads[:5]:
+        load.start()
     barrier = pltpu.get_barrier_semaphore()
     for step in Z_STEPS:
         pl.semaphore_signal(barrier, inc=1, device_id=z_peer(step)[1], device_id_type=MESH)
@@ -119,13 +132,7 @@
     for step in range(1, NG):
         pl.semaphore_signal(barrier, inc=1, device_id=g_peer(step), device_id_type=MESH)
 
-    loads = [
-        pltpu.make_async_copy(src, dst, const_sem.at[n])
-        for n, (src, dst) in enumerate(
-            ((fo_hbm, fo), (tw_hbm, tw), (fi_hbm, fi), (ii_hbm, ii), (io_hbm, io))
-        )
-    ]
-    for load in loads:
+    for load in loads[5:]:
         load.start()
 
     sends = []
@@ -141,6 +148,8 @@
     def arrived(ref, sem):
         pltpu.make_async_copy(ref, ref, sem).wait()
 
+    for load in loads[:5]:
+        load.wait()
     channels = q_ref.shape[0]
     for n, ref in enumerate((q_ref, k_ref, v_ref, g_ref)):
         stage[n * channels : (n + 1) * channels, :] = ref[...].astype(F32)
@@ -185,7 +194,9 @@
         tok[4, rows_of(other), :] = r2f[other]
 
     channel = z + NZ * pair
-    taps = [[ref[channel, j] for j in range(3)] for ref in (tq_ref, tk_ref, tv_ref)]
+    for load in loads[5:8]:
+        load.wait()
+    taps = [[ref[j, channel] for j in range(3)] for ref in (tq_ref, tk_ref, tv_ref)]
 
     def conv(value, weights):
         return weights[0] * value + weights[1] * earlier(value, 1) + weights[2] * earlier(value, 2)
@@ -196,7 +207,7 @@
     gated = key_conv * value_conv
     grad_long = grad_out * conv(tok[0], taps[0])
 
-    for load in loads:
+    for load in loads[8:]:
         load.wait()
     signals = jnp.concatenate([gated, grad_long, tok[4]], axis=1)
     outer = left_table(fo, signals)
@@ -255,44 +266,49 @@
         s4[pl.ds(NI + i, NZ, stride=16), :] = r3[2 * i + 1, 0]
         s4[pl.ds(2 * NI + i, NZ, stride=16), :] = r3[2 * i + 1, 1]
     s4[pl.ds(12, NZ, stride=16), :] = (r3[0, 1] + r3[2, 1]) + (r3[4, 1] + r3[6, 1])
-    for other in range(3):
-        s4[pl.ds(13 + other, NZ, stride=16), :] = jnp.zeros((NZ, BLK), F32)
-    my_rows = pl.ds(pl.multiple_of(z * 16, 16), 16)
+    my_rows = pl.ds(pl.multiple_of(z * 16, 16), 13)
     for n, step in enumerate(Z_STEPS):
         other, target = z_peer(step)
-        rows = pl.ds(pl.multiple_of(other * 16, 16), 16)
+        rows = pl.ds(pl.multiple_of(other * 16, 16), 13)
         send(s4.at[rows], r4.at[my_rows], c_send.at[n], c_recv, target)
     r4[my_rows, :] = s4[my_rows, :]
-    arrived(r4.at[pl.ds(0, (NZ - 1) * 16)], c_recv)
+    arrived(r4.at[pl.ds(0, (NZ - 1) * 13)], c_recv)
 
     total = jnp.sum(r4[pl.ds(12, NZ, stride=16), :], axis=0, keepdims=True)
     s5[...] = total
     for n, step in enumerate(range(1, NG)):
         send(s5, r5.at[grp], g_send.at[n], g_recv, g_peer(step))
     r5[grp] = total
-    for n, ref in enumerate((oq_ref, ok_ref, ov_ref)):
-        for i in range(NI):
-            ref[i * NZ : (i + 1) * NZ, :] = r4[pl.ds(n * NI + i, NZ, stride=16), :]
     arrived(r5.at[pl.ds(0, NG - 1)], g_recv)
     of_ref[...] = (r5[0] + r5[1]) + (r5[2] + r5[3])
     for copy in sends:
         copy.wait_send()
 
 
+def unpack(r4, total, oq_ref, ok_ref, ov_ref, of_ref):
+    for n, ref in enumerate((oq_ref, ok_ref, ov_ref)):
+        for i in range(NI):
+            ref[i * NZ : (i + 1) * NZ, :] = r4[pl.ds(n * NI + i, NZ, stride=16), :]
+    of_ref[...] = total[...]
+
+
 def local(query_branch, key_branch, value_branch, query_taps, key_taps, value_taps, long_filter, grad_out):
     channels, count = query_branch.shape
     vmem = pl.BlockSpec(memory_space=pltpu.VMEM)
-    smem = pl.BlockSpec(memory_space=pltpu.SMEM)
-    hbm = pl.BlockSpec(memory_space=pl.ANY)
+    hbm = pl.BlockSpec(memory_space=pltpu.HBM)
     consts = [jnp.asarray(table) for table in tables()]
     token_out = jax.ShapeDtypeStruct((channels, count), F32)
+    filter_out = jax.ShapeDtypeStruct((1, count), F32)
     sems = pltpu.SemaphoreType.DMA
-    outs = pl.pallas_call(
+    rows, total = pl.pallas_call(
         kernel,
-        out_shape=(token_out, token_out, token_out, jax.ShapeDtypeStruct((1, count), F32)),
-        in_specs=[vmem] * 4 + [smem] * 3 + [vmem] + [hbm] * 5,
-        out_specs=(vmem,) * 4,
-        scratch_shapes=[pltpu.VMEM(c.shape, c.dtype) for c in consts]
+        out_shape=(jax.ShapeDtypeStruct((NZ * 16, BLK), F32), filter_out),
+        in_specs=[hbm] * (8 + len(consts)),
+        out_specs=(vmem,) * 2,
+        scratch_shapes=[pltpu.VMEM((channels, count), BF16)] * 4
+        + [pltpu.VMEM((1, count), F32)]
+        + [pltpu.SMEM((3, channels), F32)] * 3
+        + [pltpu.VMEM(c.shape, c.dtype) for c in consts]
         + [
             pltpu.VMEM((4 * channels, BLK), F32),
             pltpu.VMEM((NZ, 16, BLK), BF16),
@@ -307,10 +323,9 @@
             pltpu.VMEM((NP, 2, NZ, BLK), F32),
             pltpu.VMEM((NP, 2, NZ, BLK), F32),
             pltpu.VMEM((NZ * 16, BLK), F32),
-            pltpu.VMEM((NZ * 16, BLK), F32),
             pltpu.VMEM((1, BLK), F32),
             pltpu.VMEM((NG, 1, BLK), F32),
-            sems((5,)),
+            sems((8 + len(consts),)),
             sems((NZ - 1,)), sems(()), sems((NZ - 1,)), sems(()),
             sems((NP - 1,)), sems(()), sems((NP - 1,)), sems(()),
             sems((NP - 1,)), sems(()),
@@ -318,12 +333,19 @@
             sems((NG - 1,)), sems(()),
         ],
         compiler_params=pltpu.CompilerParams(
-            collective_id=0, has_side_effects=True, vmem_limit_bytes=32 * 1024 * 1024
+            collective_id=0, has_side_effects=True, vmem_limit_bytes=56 * 1024 * 1024
         ),
     )(
-        query_branch, key_branch, value_branch, grad_out,
-        query_taps, key_taps, value_taps, long_filter.reshape(1, count), *consts,
-    )
+        query_branch, key_branch, value_branch, grad_out, long_filter.reshape(1, count),
+        query_taps.T, key_taps.T, value_taps.T, *consts,
+    )
+    outs = pl.pallas_call(
+        unpack,
+        out_shape=(token_out, token_out, token_out, filter_out),
+        in_specs=[vmem] * 2,
+        out_specs=(vmem,) * 4,
+        compiler_params=pltpu.CompilerParams(vmem_limit_bytes=4 * 1024 * 1024),
+    )(rows, total)
     return outs[0], outs[1], outs[2], outs[3].reshape(count)
 
 

time: 60.5 us -> 50.8 us (0.84)
  local copies, waits for them, and re-layouts: 9.14 us -> 1.56 us
  Pallas kernels: 50.3 us -> 48.4 us
    unnamed x31 -> x4, local copies, waits for them, and re-layouts: 9.14 us -> 1.56 us
    pallas_call x1 -> x2, Pallas kernels: 50.3 us -> 48.4 us  [the longest x1 47.7 us: local(): pl.pallas_call(kernel, out_shape=(jax.ShapeDtypeStruct((NZ * 16, BLK), F3...]
where the time goes in v2:
time: 50.8 us; the launch traced here: 50.6 us
  Pallas kernels  48.4 us (95%)
  local copies, waits for them, and re-layouts  1.56 us (3%)
  between operations  0.65 us (1%)
    pallas_call x1, Pallas kernels, local(): pl.pallas_call(kernel, out_shape=(jax.ShapeDtypeStruct((NZ * 16, BLK), F3...  47.7 us
    unnamed x4, local copies, waits for them, and re-layouts  1.56 us

profile of v2, /device:TPU:1, one launch (start us, length us, event | category | flops | bytes accessed | tf_op | source)
XLA Modules:
  0.0 50.6 jit_solution(1642236368576406619)
XLA Ops:
  0.6 47.7 %shard_map.156 = (f32[256,128]{1,0:T(8,128)}, f32[1,128]{1,0:T(1,128)}) custom-call(bf16[64,128]{1,0:T(8,128)(2,1)} %q_hbm.1, bf16[64,128]{1,0:T(8,128)(2,1)} %k_hbm.1, bf16[64,128]{1,0:T(8,128)(2,1)} %v_hbm.1, bf16[64,128]{1,0:T(8,128)(2,1)} %g_hbm.1, f32[1,128]{1,0:T(1,128)} %bitcast.8, f32[3,64]{1,0:T(4,128)} %bitcast.5, f32[3,64]{1,0:T(4,128)} %bitcast.6, ...), custom_call_target="tpu_custom_call" | custom-call | tf_op jit(solution)/shard_map/pallas_call | solution.py:303
  48.4 0.0 copy-start.1
  48.4 0.7 %copy-done.1 = f32[1,128]{1,0:T(1,128)S(1)} copy-done((f32[1,128]{1,0:T(1,128)S(1)}, f32[1,128]{1,0:T(1,128)}, u32[]{:S(2)}) %copy-start.1) | copy-done | bytes 536
  49.0 0.0 copy-start
  49.0 0.9 %copy-done = f32[256,128]{1,0:T(8,128)S(1)} copy-done((f32[256,128]{1,0:T(8,128)S(1)}, f32[256,128]{1,0:T(8,128)}, u32[]{:S(2)}) %copy-start) | copy-done | bytes 131096
  50.0 0.7 %shard_map.157 = (f32[64,128]{1,0:T(8,128)}, f32[64,128]{1,0:T(8,128)}, f32[64,128]{1,0:T(8,128)}, f32[1,128]{1,0:T(1,128)}) custom-call(f32[256,128]{1,0:T(8,128)S(1)} %copy-done, f32[1,128]{1,0:T(1,128)S(1)} %copy-done.1), custom_call_target="tpu_custom_call" | custom-call | tf_op jit(solution)/shard_map/pallas_call | solution.py:342
Async XLA Ops:
  48.4 0.7 %copy-start.1 = (f32[1,128]{1,0:T(1,128)S(1)}, f32[1,128]{1,0:T(1,128)}, u32[]{:S(2)}) copy-start(f32[1,128]{1,0:T(1,128)} %get-tuple-element.11.total) | copy-start | bytes 1540
  49.0 0.9 %copy-start = (f32[256,128]{1,0:T(8,128)S(1)}, f32[256,128]{1,0:T(8,128)}, u32[]{:S(2)}) copy-start(f32[256,128]{1,0:T(8,128)} %get-tuple-element.10.r4) | copy-start | bytes 393220

commit v3 on v2

--- a/solution.py
+++ b/solution.py
@@ -88,12 +88,12 @@
 def kernel(
     q_hbm, k_hbm, v_hbm, g_hbm, filt_hbm, tq_hbm, tk_hbm, tv_hbm,
     fo_hbm, tw_hbm, fi_hbm, ii_hbm, io_hbm,
-    r4, of_ref,
+    r4_hbm, of_ref,
     q_ref, k_ref, v_ref, g_ref, filt_ref, tq_ref, tk_ref, tv_ref,
     fo, tw, fi, ii, io,
-    stage, s1, r1, r1f, s2, r2, s2f, r2f, tok, res, s3, r3, s4, s5, r5,
+    stage, s1, r1, r1f, s2, r2, s2f, r2f, tok, res, s3, r3, s4, s4f, r4f, s5, r5,
     load_sem, z_send, z_recv, zf_send, zf_recv, p_send, p_recv, pf_send, pf_recv,
-    b_send, b_recv, c_send, c_recv, g_send, g_recv,
+    b_send, b_recv, c_send, c_recv, cf_send, cf_recv, own_sem, g_send, g_recv,
 ):
     me = lax.axis_index("ctx")
     grp = lax.axis_index("grp")
@@ -135,15 +135,12 @@
     for load in loads[5:]:
         load.start()
 
-    sends = []
-
     def send(src, dst, send_sem, recv_sem, target):
         copy = pltpu.make_async_remote_copy(
             src_ref=src, dst_ref=dst, send_sem=send_sem, recv_sem=recv_sem,
             device_id=target, device_id_type=MESH,
         )
         copy.start()
-        sends.append(copy)
 
     def arrived(ref, sem):
         pltpu.make_async_copy(ref, ref, sem).wait()
@@ -157,12 +154,12 @@
         s1[other] = stage[pl.ds(other, 16, stride=NZ), :].astype(BF16)
     pl.semaphore_wait(barrier, len(Z_STEPS) + NP - 1 + NG - 1)
 
-    for n, step in enumerate(Z_STEPS):
+    for step in Z_STEPS:
         other, target = z_peer(step)
-        send(s1.at[other], r1.at[z], z_send.at[n], z_recv, target)
-    for n, step in enumerate(Z_STEPS):
+        send(s1.at[other], r1.at[z], z_send, z_recv, target)
+    for step in Z_STEPS:
         other, target = z_peer(step)
-        send(filt_ref, r1f.at[z], zf_send.at[n], zf_recv, target)
+        send(filt_ref, r1f.at[z], zf_send, zf_recv, target)
     r1[z] = s1[z]
     r1f[z] = filt_ref[...]
     arrived(r1.at[pl.ds(0, NZ - 1)], z_recv)
@@ -171,14 +168,16 @@
     for i in range(NI):
         for n in range(4):
             s2[i, n] = stage[pl.ds(n * NI + i, NZ, stride=16), :].astype(BF16)
-    for n, step in enumerate(range(1, NP)):
+    for step in range(1, NP):
         other, target = p_peer(step)
-        send(s2.at[other // 2], r2.at[p], p_send.at[n], p_recv, target)
+        send(s2.at[other // 2], r2.at[p], p_send, p_recv, target)
+    arrived(r1.at[pl.ds(0, NZ - 1)], z_send)
+    arrived(r1f.at[pl.ds(0, NZ - 1)], zf_send)
     arrived(r1f.at[pl.ds(0, NZ - 1)], zf_recv)
     s2f[...] = r1f[...].reshape(NZ, BLK)
-    for n, step in enumerate(range(1, NP)):
+    for step in range(1, NP):
         other, target = p_peer(step)
-        send(s2f, r2f.at[p], pf_send.at[n], pf_recv, target)
+        send(s2f, r2f.at[p], pf_send, pf_recv, target)
     r2[p] = s2[pair]
     r2f[p] = s2f[...]
     arrived(r2.at[pl.ds(0, NP - 1)], p_recv)
@@ -255,41 +254,60 @@
     for other in range(NP):
         for n in range(2):
             s3[other, n] = res[n, rows_of(other), :]
-    for n, step in enumerate(range(1, NP)):
+    for step in range(1, NP):
         other, target = p_peer(step)
-        send(s3.at[other], r3.at[p], b_send.at[n], b_recv, target)
+        send(s3.at[other], r3.at[p], b_send, b_recv, target)
     r3[p] = s3[p]
     arrived(r3.at[pl.ds(0, NP - 1)], b_recv)
 
+    s4f[...] = ((r3[0, 1] + r3[2, 1]) + (r3[4, 1] + r3[6, 1])).reshape(NZ, 1, BLK)
+    for step in Z_STEPS:
+        other, target = z_peer(step)
+        send(s4f.at[other], r4f.at[z], cf_send, cf_recv, target)
     for i in range(NI):
         s4[pl.ds(i, NZ, stride=16), :] = r3[2 * i, 0]
         s4[pl.ds(NI + i, NZ, stride=16), :] = r3[2 * i + 1, 0]
         s4[pl.ds(2 * NI + i, NZ, stride=16), :] = r3[2 * i + 1, 1]
-    s4[pl.ds(12, NZ, stride=16), :] = (r3[0, 1] + r3[2, 1]) + (r3[4, 1] + r3[6, 1])
-    my_rows = pl.ds(pl.multiple_of(z * 16, 16), 13)
-    for n, step in enumerate(Z_STEPS):
+    my_rows = pl.ds(pl.multiple_of(z * 16, 16), 12)
+    for step in Z_STEPS:
         other, target = z_peer(step)
-        rows = pl.ds(pl.multiple_of(other * 16, 16), 13)
-        send(s4.at[rows], r4.at[my_rows], c_send.at[n], c_recv, target)
-    r4[my_rows, :] = s4[my_rows, :]
-    arrived(r4.at[pl.ds(0, (NZ - 1) * 13)], c_recv)
-
-    total = jnp.sum(r4[pl.ds(12, NZ, stride=16), :], axis=0, keepdims=True)
+        rows = pl.ds(pl.multiple_of(other * 16, 16), 12)
+        send(s4.at[rows], r4_hbm.at[my_rows], c_send, c_recv, target)
+    own = pltpu.make_async_copy(s4.at[my_rows], r4_hbm.at[my_rows], own_sem)
+    own.start()
+    r4f[z] = s4f[z]
+    arrived(r2.at[pl.ds(0, NP - 1)], p_send)
+    arrived(r2f.at[pl.ds(0, NP - 1)], pf_send)
+    arrived(r3.at[pl.ds(0, NP - 1)], b_send)
+    arrived(r4f.at[pl.ds(0, NZ - 1)], cf_send)
+    arrived(r4f.at[pl.ds(0, NZ - 1)], cf_recv)
+
+    total = jnp.sum(r4f[...].reshape(NZ, BLK), axis=0, keepdims=True)
     s5[...] = total
-    for n, step in enumerate(range(1, NG)):
-        send(s5, r5.at[grp], g_send.at[n], g_recv, g_peer(step))
+    for step in range(1, NG):
+        send(s5, r5.at[grp], g_send, g_recv, g_peer(step))
     r5[grp] = total
+    own.wait()
+    arrived(r5.at[pl.ds(0, NG - 1)], g_send)
     arrived(r5.at[pl.ds(0, NG - 1)], g_recv)
     of_ref[...] = (r5[0] + r5[1]) + (r5[2] + r5[3])
-    for copy in sends:
-        copy.wait_send()
-
-
-def unpack(r4, total, oq_ref, ok_ref, ov_ref, of_ref):
+    arrived(s4.at[pl.ds(0, (NZ - 1) * 12)], c_send)
+    arrived(s4.at[pl.ds(0, (NZ - 1) * 12)], c_recv)
+
+
+def unpack(r4, total, oq_ref, ok_ref, ov_ref, of_ref, sem):
+    copies = [pltpu.make_async_copy(total, of_ref, sem.at[3 * NI])]
     for n, ref in enumerate((oq_ref, ok_ref, ov_ref)):
         for i in range(NI):
-            ref[i * NZ : (i + 1) * NZ, :] = r4[pl.ds(n * NI + i, NZ, stride=16), :]
-    of_ref[...] = total[...]
+            copies.append(
+                pltpu.make_async_copy(
+                    r4.at[:, n * NI + i, :], ref.at[pl.ds(i * NZ, NZ)], sem.at[n * NI + i]
+                )
+            )
+    for copy in copies:
+        copy.start()
+    for copy in copies:
+        copy.wait()
 
 
 def local(query_branch, key_branch, value_branch, query_taps, key_taps, value_taps, long_filter, grad_out):
@@ -304,7 +322,7 @@
         kernel,
         out_shape=(jax.ShapeDtypeStruct((NZ * 16, BLK), F32), filter_out),
         in_specs=[hbm] * (8 + len(consts)),
-        out_specs=(vmem,) * 2,
+        out_specs=(hbm, vmem),
         scratch_shapes=[pltpu.VMEM((channels, count), BF16)] * 4
         + [pltpu.VMEM((1, count), F32)]
         + [pltpu.SMEM((3, channels), F32)] * 3
@@ -323,15 +341,13 @@
             pltpu.VMEM((NP, 2, NZ, BLK), F32),
             pltpu.VMEM((NP, 2, NZ, BLK), F32),
             pltpu.VMEM((NZ * 16, BLK), F32),
+            pltpu.VMEM((NZ, 1, BLK), F32),
+            pltpu.VMEM((NZ, 1, BLK), F32),
             pltpu.VMEM((1, BLK), F32),
             pltpu.VMEM((NG, 1, BLK), F32),
             sems((8 + len(consts),)),
-            sems((NZ - 1,)), sems(()), sems((NZ - 1,)), sems(()),
-            sems((NP - 1,)), sems(()), sems((NP - 1,)), sems(()),
-            sems((NP - 1,)), sems(()),
-            sems((NZ - 1,)), sems(()),
-            sems((NG - 1,)), sems(()),
-        ],
+        ]
+        + [sems(())] * 17,
         compiler_params=pltpu.CompilerParams(
             collective_id=0, has_side_effects=True, vmem_limit_bytes=56 * 1024 * 1024
         ),
@@ -342,10 +358,11 @@
     outs = pl.pallas_call(
         unpack,
         out_shape=(token_out, token_out, token_out, filter_out),
-        in_specs=[vmem] * 2,
-        out_specs=(vmem,) * 4,
-        compiler_params=pltpu.CompilerParams(vmem_limit_bytes=4 * 1024 * 1024),
-    )(rows, total)
+        in_specs=[hbm] * 2,
+        out_specs=(hbm,) * 4,
+        scratch_shapes=[sems((3 * NI + 1,))],
+        compiler_params=pltpu.CompilerParams(vmem_limit_bytes=56 * 1024 * 1024),
+    )(rows.reshape(NZ, 16, BLK), total)
     return outs[0], outs[1], outs[2], outs[3].reshape(count)
 
 

time: 50.8 us -> 51.9 us (1.022)
  Pallas kernels: 48.4 us -> 51.1 us
  local copies, waits for them, and re-layouts: 1.56 us -> 0 us
    pallas_call x1, Pallas kernels: 0.67 us -> 4.22 us  [local(): pl.pallas_call(unpack, out_shape=(token_out, token_out, token_out, filter...]
    unnamed x4 -> x0, local copies, waits for them, and re-layouts: 1.56 us -> none
    pallas_call x1, Pallas kernels: 47.7 us -> 46.9 us  [local(): pl.pallas_call(kernel, out_shape=(jax.ShapeDtypeStruct((NZ * 16, BLK), F3...]
where the time goes in v3:
time: 51.9 us; the launch traced here: 51.7 us
  Pallas kernels  51.1 us (98%)
  between operations  0.64 us (1%)
    pallas_call x1, Pallas kernels, local(): pl.pallas_call(kernel, out_shape=(jax.ShapeDtypeStruct((NZ * 16, BLK), F3...  46.9 us
    pallas_call x1, Pallas kernels, local(): pl.pallas_call(unpack, out_shape=(token_out, token_out, token_out, filter...  4.22 us

profile of v3, /device:TPU:1, one launch (start us, length us, event | category | flops | bytes accessed | tf_op | source)
XLA Modules:
  0.0 51.7 jit_solution(6697913465522631033)
XLA Ops:
  0.6 46.9 %shard_map.156 = (f32[256,128]{1,0:T(8,128)}, f32[1,128]{1,0:T(1,128)}) custom-call(bf16[64,128]{1,0:T(8,128)(2,1)} %q_hbm.1, bf16[64,128]{1,0:T(8,128)(2,1)} %k_hbm.1, bf16[64,128]{1,0:T(8,128)(2,1)} %v_hbm.1, bf16[64,128]{1,0:T(8,128)(2,1)} %g_hbm.1, f32[1,128]{1,0:T(1,128)} %bitcast.10, f32[3,64]{1,0:T(4,128)} %bitcast.7, f32[3,64]{1,0:T(4,128)} %bitcast.8, ...), custom_call_target="tpu_custom_call" | custom-call | tf_op jit(solution)/shard_map/pallas_call | solution.py:321
  47.5 4.2 %shard_map.157 = (f32[64,128]{1,0:T(8,128)}, f32[64,128]{1,0:T(8,128)}, f32[64,128]{1,0:T(8,128)}, f32[1,128]{1,0:T(1,128)}) custom-call(f32[16,16,128]{2,1,0:T(8,128)} %bitcast.6, f32[1,128]{1,0:T(1,128)} %get-tuple-element.11.total), custom_call_target="tpu_custom_call" | custom-call | tf_op jit(solution)/shard_map/pallas_call | solution.py:358

commit v4 on v3

--- a/solution.py
+++ b/solution.py
@@ -88,12 +88,12 @@
 def kernel(
     q_hbm, k_hbm, v_hbm, g_hbm, filt_hbm, tq_hbm, tk_hbm, tv_hbm,
     fo_hbm, tw_hbm, fi_hbm, ii_hbm, io_hbm,
-    r4_hbm, of_ref,
+    oq_hbm, ok_hbm, ov_hbm, of_ref,
     q_ref, k_ref, v_ref, g_ref, filt_ref, tq_ref, tk_ref, tv_ref,
     fo, tw, fi, ii, io,
-    stage, s1, r1, r1f, s2, r2, s2f, r2f, tok, res, s3, r3, s4, s4f, r4f, s5, r5,
+    stage, s1, r1, r1f, s2, r2, s2f, r2f, tok, res, s3, r3, s4, r4, out, s4f, r4f, s5, r5,
     load_sem, z_send, z_recv, zf_send, zf_recv, p_send, p_recv, pf_send, pf_recv,
-    b_send, b_recv, c_send, c_recv, cf_send, cf_recv, own_sem, g_send, g_recv,
+    b_send, b_recv, c_send, c_recv, cf_send, cf_recv, out_sem, g_send, g_recv,
 ):
     me = lax.axis_index("ctx")
     grp = lax.axis_index("grp")
@@ -272,9 +272,8 @@
     for step in Z_STEPS:
         other, target = z_peer(step)
         rows = pl.ds(pl.multiple_of(other * 16, 16), 12)
-        send(s4.at[rows], r4_hbm.at[my_rows], c_send, c_recv, target)
-    own = pltpu.make_async_copy(s4.at[my_rows], r4_hbm.at[my_rows], own_sem)
-    own.start()
+        send(s4.at[rows], r4.at[my_rows], c_send, c_recv, target)
+    r4[my_rows, :] = s4[my_rows, :]
     r4f[z] = s4f[z]
     arrived(r2.at[pl.ds(0, NP - 1)], p_send)
     arrived(r2f.at[pl.ds(0, NP - 1)], pf_send)
@@ -287,27 +286,27 @@
     for step in range(1, NG):
         send(s5, r5.at[grp], g_send, g_recv, g_peer(step))
     r5[grp] = total
-    own.wait()
+    arrived(r4.at[pl.ds(0, (NZ - 1) * 12)], c_recv)
+    for n in range(3):
+        for i in range(NI):
+            out[n, i * NZ : (i + 1) * NZ, :] = r4[pl.ds(n * NI + i, NZ, stride=16), :]
+    stores = [
+        pltpu.make_async_copy(out.at[n], ref, out_sem.at[n])
+        for n, ref in enumerate((oq_hbm, ok_hbm, ov_hbm))
+    ]
+    for store in stores:
+        store.start()
+    arrived(s4.at[pl.ds(0, (NZ - 1) * 12)], c_send)
     arrived(r5.at[pl.ds(0, NG - 1)], g_send)
     arrived(r5.at[pl.ds(0, NG - 1)], g_recv)
     of_ref[...] = (r5[0] + r5[1]) + (r5[2] + r5[3])
-    arrived(s4.at[pl.ds(0, (NZ - 1) * 12)], c_send)
-    arrived(s4.at[pl.ds(0, (NZ - 1) * 12)], c_recv)
-
-
-def unpack(r4, total, oq_ref, ok_ref, ov_ref, of_ref, sem):
-    copies = [pltpu.make_async_copy(total, of_ref, sem.at[3 * NI])]
-    for n, ref in enumerate((oq_ref, ok_ref, ov_ref)):
-        for i in range(NI):
-            copies.append(
-                pltpu.make_async_copy(
-                    r4.at[:, n * NI + i, :], ref.at[pl.ds(i * NZ, NZ)], sem.at[n * NI + i]
-                )
-            )
-    for copy in copies:
-        copy.start()
-    for copy in copies:
-        copy.wait()
+    for store in stores:
+        store.wait()
+
+
+def passed(*refs):
+    for source, target in zip(refs[:4], refs[4:]):
+        target[...] = source[...]
 
 
 def local(query_branch, key_branch, value_branch, query_taps, key_taps, value_taps, long_filter, grad_out):
@@ -318,11 +317,11 @@
     token_out = jax.ShapeDtypeStruct((channels, count), F32)
     filter_out = jax.ShapeDtypeStruct((1, count), F32)
     sems = pltpu.SemaphoreType.DMA
-    rows, total = pl.pallas_call(
+    made = pl.pallas_call(
         kernel,
-        out_shape=(jax.ShapeDtypeStruct((NZ * 16, BLK), F32), filter_out),
+        out_shape=(token_out, token_out, token_out, filter_out),
         in_specs=[hbm] * (8 + len(consts)),
-        out_specs=(hbm, vmem),
+        out_specs=(hbm, hbm, hbm, vmem),
         scratch_shapes=[pltpu.VMEM((channels, count), BF16)] * 4
         + [pltpu.VMEM((1, count), F32)]
         + [pltpu.SMEM((3, channels), F32)] * 3
@@ -341,13 +340,16 @@
             pltpu.VMEM((NP, 2, NZ, BLK), F32),
             pltpu.VMEM((NP, 2, NZ, BLK), F32),
             pltpu.VMEM((NZ * 16, BLK), F32),
+            pltpu.VMEM((NZ * 16, BLK), F32),
+            pltpu.VMEM((3, channels, BLK), F32),
             pltpu.VMEM((NZ, 1, BLK), F32),
             pltpu.VMEM((NZ, 1, BLK), F32),
             pltpu.VMEM((1, BLK), F32),
             pltpu.VMEM((NG, 1, BLK), F32),
             sems((8 + len(consts),)),
         ]
-        + [sems(())] * 17,
+        + [sems(())] * 14
+        + [sems((3,)), sems(()), sems(())],
         compiler_params=pltpu.CompilerParams(
             collective_id=0, has_side_effects=True, vmem_limit_bytes=56 * 1024 * 1024
         ),
@@ -356,13 +358,12 @@
         query_taps.T, key_taps.T, value_taps.T, *consts,
     )
     outs = pl.pallas_call(
-        unpack,
+        passed,
         out_shape=(token_out, token_out, token_out, filter_out),
-        in_specs=[hbm] * 2,
-        out_specs=(hbm,) * 4,
-        scratch_shapes=[sems((3 * NI + 1,))],
+        in_specs=[vmem] * 4,
+        out_specs=(vmem,) * 4,
         compiler_params=pltpu.CompilerParams(vmem_limit_bytes=56 * 1024 * 1024),
-    )(rows.reshape(NZ, 16, BLK), total)
+    )(*made)
     return outs[0], outs[1], outs[2], outs[3].reshape(count)
 
 

time: 51.9 us -> 49.2 us (0.948)
  Pallas kernels: 51.1 us -> 48.3 us
    pallas_call x2, Pallas kernels: 51.1 us -> 48.3 us  [the longest x1 46.8 us: local(): pl.pallas_call(kernel, out_shape=(token_out, token_out, token_out, filter...]
where the time goes in v4:
time: 49.2 us; the launch traced here: 48.9 us
  Pallas kernels  48.3 us (98%)
  between operations  0.64 us (1%)
    pallas_call x1, Pallas kernels, local(): pl.pallas_call(kernel, out_shape=(token_out, token_out, token_out, filter...  46.8 us
    pallas_call x1, Pallas kernels, local(): pl.pallas_call(passed, out_shape=(token_out, token_out, token_out, filter...  1.44 us

profile of v4, /device:TPU:1, one launch (start us, length us, event | category | flops | bytes accessed | tf_op | source)
XLA Modules:
  0.0 48.9 jit_solution(9983927984279836993)
XLA Ops:
  0.6 46.8 %shard_map.156 = (f32[64,128]{1,0:T(8,128)}, f32[64,128]{1,0:T(8,128)}, f32[64,128]{1,0:T(8,128)}, f32[1,128]{1,0:T(1,128)}) custom-call(bf16[64,128]{1,0:T(8,128)(2,1)} %q_hbm.1, bf16[64,128]{1,0:T(8,128)(2,1)} %k_hbm.1, bf16[64,128]{1,0:T(8,128)(2,1)} %v_hbm.1, bf16[64,128]{1,0:T(8,128)(2,1)} %g_hbm.1, f32[1,128]{1,0:T(1,128)} %bitcast.8, ...), custom_call_target="tpu_custom_call" | custom-call | tf_op jit(solution)/shard_map/pallas_call | solution.py:320
  47.5 1.4 %shard_map.157 = (f32[64,128]{1,0:T(8,128)}, f32[64,128]{1,0:T(8,128)}, f32[64,128]{1,0:T(8,128)}, f32[1,128]{1,0:T(1,128)}) custom-call(f32[64,128]{1,0:T(8,128)} %get-tuple-element.12.refs_0_, f32[64,128]{1,0:T(8,128)} %get-tuple-element.13.refs_1_, f32[64,128]{1,0:T(8,128)} %get-tuple-element.14.refs_2_, f32[1,128]{1,0:T(1,128)} %get-tuple-element.15.refs_3_), custom_call_target="tpu_custom_call" | custom-call | tf_op jit(solution)/shard_map/pallas_call | solution.py:360

commit v5 on v4

--- a/solution.py
+++ b/solution.py
@@ -18,6 +18,7 @@
 FULL = 2 * BLK * NB
 MESH = pl.DeviceIdType.MESH
 Z_STEPS = (8, 7, 9, 6, 10, 5, 11, 4, 12, 3, 13, 2, 14, 1, 15)
+ZG_STEPS = [(step, turn) for step in Z_STEPS + (0,) for turn in range(NG) if step or turn]
 F32, BF16 = jnp.float32, jnp.bfloat16
 
 
@@ -88,12 +89,12 @@
 def kernel(
     q_hbm, k_hbm, v_hbm, g_hbm, filt_hbm, tq_hbm, tk_hbm, tv_hbm,
     fo_hbm, tw_hbm, fi_hbm, ii_hbm, io_hbm,
-    oq_hbm, ok_hbm, ov_hbm, of_ref,
+    oq_ref, ok_ref, ov_ref, of_ref,
     q_ref, k_ref, v_ref, g_ref, filt_ref, tq_ref, tk_ref, tv_ref,
     fo, tw, fi, ii, io,
-    stage, s1, r1, r1f, s2, r2, s2f, r2f, tok, res, s3, r3, s4, r4, out, s4f, r4f, s5, r5,
-    load_sem, z_send, z_recv, zf_send, zf_recv, p_send, p_recv, pf_send, pf_recv,
-    b_send, b_recv, c_send, c_recv, cf_send, cf_recv, out_sem, g_send, g_recv,
+    stage, s1, r1, f1, s2, r2, f2, tok, res, s3, r3, s4, r4, s4f, r4f,
+    load_sem, z_send, z_recv, f1_send, f1_recv, p_send, p_recv, f2_send, f2_recv,
+    b_send, b_recv, c_send, c_recv, cf_send, cf_recv,
 ):
     me = lax.axis_index("ctx")
     grp = lax.axis_index("grp")
@@ -105,12 +106,13 @@
         other = (z + step) % NZ
         return other, {"ctx": (y * NZ + other) * NX + x}
 
+    def zg_peer(step, turn):
+        other, target = z_peer(step)
+        return other, {**target, "grp": (grp + turn) % NG}
+
     def p_peer(step):
         other = (p + step) % NP
         return other, {"ctx": ((other // NX) * NZ + z) * NX + other % NX}
-
-    def g_peer(step):
-        return {"grp": (grp + step) % NG}
 
     loads = [
         pltpu.make_async_copy(src, dst, load_sem.at[n])
@@ -125,12 +127,10 @@
     for load in loads[:5]:
         load.start()
     barrier = pltpu.get_barrier_semaphore()
-    for step in Z_STEPS:
-        pl.semaphore_signal(barrier, inc=1, device_id=z_peer(step)[1], device_id_type=MESH)
-    for step in range(1, NP):
-        pl.semaphore_signal(barrier, inc=1, device_id=p_peer(step)[1], device_id_type=MESH)
-    for step in range(1, NG):
-        pl.semaphore_signal(barrier, inc=1, device_id=g_peer(step), device_id_type=MESH)
+    targets = [zg_peer(step, turn)[1] for step, turn in ZG_STEPS]
+    targets += [p_peer(step)[1] for step in range(1, NP)]
+    for target in targets:
+        pl.semaphore_signal(barrier, inc=1, device_id=target, device_id_type=MESH)
 
     for load in loads[5:]:
         load.start()
@@ -152,16 +152,20 @@
         stage[n * channels : (n + 1) * channels, :] = ref[...].astype(F32)
     for other in range(NZ):
         s1[other] = stage[pl.ds(other, 16, stride=NZ), :].astype(BF16)
-    pl.semaphore_wait(barrier, len(Z_STEPS) + NP - 1 + NG - 1)
+    f1[p] = filt_ref[...]
+    pl.semaphore_wait(barrier, len(targets))
+
+    for step in range(1, NP):
+        send(filt_ref, f1.at[p], f1_send, f1_recv, p_peer(step)[1])
 
     for step in Z_STEPS:
         other, target = z_peer(step)
         send(s1.at[other], r1.at[z], z_send, z_recv, target)
+    r1[z] = s1[z]
+    arrived(f1.at[pl.ds(0, NP - 1)], f1_recv)
     for step in Z_STEPS:
-        other, target = z_peer(step)
-        send(filt_ref, r1f.at[z], zf_send, zf_recv, target)
-    r1[z] = s1[z]
-    r1f[z] = filt_ref[...]
+        send(f1, f2.at[z], f2_send, f2_recv, z_peer(step)[1])
+    f2[z] = f1[...]
     arrived(r1.at[pl.ds(0, NZ - 1)], z_recv)
 
     stage[...] = r1[...].astype(F32).reshape(NZ * 16, BLK)
@@ -171,15 +175,36 @@
     for step in range(1, NP):
         other, target = p_peer(step)
         send(s2.at[other // 2], r2.at[p], p_send, p_recv, target)
+    r2[p] = s2[pair]
+    arrived(f1.at[pl.ds(0, NP - 1)], f1_send)
     arrived(r1.at[pl.ds(0, NZ - 1)], z_send)
-    arrived(r1f.at[pl.ds(0, NZ - 1)], zf_send)
-    arrived(r1f.at[pl.ds(0, NZ - 1)], zf_recv)
-    s2f[...] = r1f[...].reshape(NZ, BLK)
-    for step in range(1, NP):
-        other, target = p_peer(step)
-        send(s2f, r2f.at[p], pf_send, pf_recv, target)
-    r2[p] = s2[pair]
-    r2f[p] = s2f[...]
+    arrived(f2.at[pl.ds(0, NZ - 1)], f2_send)
+    arrived(f2.at[pl.ds(0, NZ - 1)], f2_recv)
+    blocks = f2[...].reshape(NB, BLK)
+    for other in range(NZ):
+        for n in range(NY):
+            row = (other * NY + n) * NX
+            to = (n * NZ + other) * NX
+            tok[4, to : to + NX, :] = blocks[row : row + NX]
+    for load in loads[5:]:
+        load.wait()
+    cos, sin = tw[0], tw[1]
+
+    def spectra(*values):
+        outer = left_table(fo, jnp.concatenate(values, axis=1))
+        turned = []
+        for n in range(len(values)):
+            re = outer[:NB, n * BLK : (n + 1) * BLK]
+            im = outer[NB:, n * BLK : (n + 1) * BLK]
+            turned.append(jnp.concatenate([re * cos + im * sin, im * cos - re * sin], axis=1))
+        both = right_table(jnp.concatenate(turned, axis=0), fi)
+        pieces = [both[n * NB : (n + 1) * NB] for n in range(len(values))]
+        return [(piece[:, :BLK], piece[:, BLK:]) for piece in pieces]
+
+    (filt_re, filt_im), = spectra(tok[4])
+    channel = z + NZ * pair
+    taps = [[ref[j, channel] for j in range(3)] for ref in (tq_ref, tk_ref, tv_ref)]
+
     arrived(r2.at[pl.ds(0, NP - 1)], p_recv)
 
     def rows_of(other):
@@ -188,14 +213,6 @@
     for other in range(NP):
         for n in range(4):
             tok[n, rows_of(other), :] = r2[other, n].astype(F32)
-    arrived(r2f.at[pl.ds(0, NP - 1)], pf_recv)
-    for other in range(NP):
-        tok[4, rows_of(other), :] = r2f[other]
-
-    channel = z + NZ * pair
-    for load in loads[5:8]:
-        load.wait()
-    taps = [[ref[j, channel] for j in range(3)] for ref in (tq_ref, tk_ref, tv_ref)]
 
     def conv(value, weights):
         return weights[0] * value + weights[1] * earlier(value, 1) + weights[2] * earlier(value, 2)
@@ -206,20 +223,7 @@
     gated = key_conv * value_conv
     grad_long = grad_out * conv(tok[0], taps[0])
 
-    for load in loads[8:]:
-        load.wait()
-    signals = jnp.concatenate([gated, grad_long, tok[4]], axis=1)
-    outer = left_table(fo, signals)
-    cos, sin = tw[0], tw[1]
-    turned = []
-    for n in range(3):
-        re = outer[:NB, n * BLK : (n + 1) * BLK]
-        im = outer[NB:, n * BLK : (n + 1) * BLK]
-        turned.append(jnp.concatenate([re * cos + im * sin, im * cos - re * sin], axis=1))
-    spectra = right_table(jnp.concatenate(turned, axis=0), fi)
-    gated_re, gated_im = spectra[:NB, :BLK], spectra[:NB, BLK:]
-    grad_re, grad_im = spectra[NB : 2 * NB, :BLK], spectra[NB : 2 * NB, BLK:]
-    filt_re, filt_im = spectra[2 * NB :, :BLK], spectra[2 * NB :, BLK:]
+    (gated_re, gated_im), (grad_re, grad_im) = spectra(gated, grad_long)
 
     first = role == 0
     left_re = jnp.where(first, gated_re, grad_re)
@@ -261,9 +265,9 @@
     arrived(r3.at[pl.ds(0, NP - 1)], b_recv)
 
     s4f[...] = ((r3[0, 1] + r3[2, 1]) + (r3[4, 1] + r3[6, 1])).reshape(NZ, 1, BLK)
-    for step in Z_STEPS:
-        other, target = z_peer(step)
-        send(s4f.at[other], r4f.at[z], cf_send, cf_recv, target)
+    for step, turn in ZG_STEPS:
+        other, target = zg_peer(step, turn)
+        send(s4f.at[other], r4f.at[z * NG + grp], cf_send, cf_recv, target)
     for i in range(NI):
         s4[pl.ds(i, NZ, stride=16), :] = r3[2 * i, 0]
         s4[pl.ds(NI + i, NZ, stride=16), :] = r3[2 * i + 1, 0]
@@ -274,34 +278,17 @@
         rows = pl.ds(pl.multiple_of(other * 16, 16), 12)
         send(s4.at[rows], r4.at[my_rows], c_send, c_recv, target)
     r4[my_rows, :] = s4[my_rows, :]
-    r4f[z] = s4f[z]
+    r4f[z * NG + grp] = s4f[z]
     arrived(r2.at[pl.ds(0, NP - 1)], p_send)
-    arrived(r2f.at[pl.ds(0, NP - 1)], pf_send)
     arrived(r3.at[pl.ds(0, NP - 1)], b_send)
-    arrived(r4f.at[pl.ds(0, NZ - 1)], cf_send)
-    arrived(r4f.at[pl.ds(0, NZ - 1)], cf_recv)
-
-    total = jnp.sum(r4f[...].reshape(NZ, BLK), axis=0, keepdims=True)
-    s5[...] = total
-    for step in range(1, NG):
-        send(s5, r5.at[grp], g_send, g_recv, g_peer(step))
-    r5[grp] = total
+    arrived(r4f.at[pl.ds(0, NZ * NG - 1)], cf_send)
+    arrived(r4f.at[pl.ds(0, NZ * NG - 1)], cf_recv)
+    of_ref[...] = jnp.sum(r4f[...].reshape(NZ * NG, BLK), axis=0, keepdims=True)
     arrived(r4.at[pl.ds(0, (NZ - 1) * 12)], c_recv)
-    for n in range(3):
+    for n, ref in enumerate((oq_ref, ok_ref, ov_ref)):
         for i in range(NI):
-            out[n, i * NZ : (i + 1) * NZ, :] = r4[pl.ds(n * NI + i, NZ, stride=16), :]
-    stores = [
-        pltpu.make_async_copy(out.at[n], ref, out_sem.at[n])
-        for n, ref in enumerate((oq_hbm, ok_hbm, ov_hbm))
-    ]
-    for store in stores:
-        store.start()
+            ref[i * NZ : (i + 1) * NZ, :] = r4[pl.ds(n * NI + i, NZ, stride=16), :]
     arrived(s4.at[pl.ds(0, (NZ - 1) * 12)], c_send)
-    arrived(r5.at[pl.ds(0, NG - 1)], g_send)
-    arrived(r5.at[pl.ds(0, NG - 1)], g_recv)
-    of_ref[...] = (r5[0] + r5[1]) + (r5[2] + r5[3])
-    for store in stores:
-        store.wait()
 
 
 def passed(*refs):
@@ -317,11 +304,15 @@
     token_out = jax.ShapeDtypeStruct((channels, count), F32)
     filter_out = jax.ShapeDtypeStruct((1, count), F32)
     sems = pltpu.SemaphoreType.DMA
+    args = [
+        query_branch, key_branch, value_branch, grad_out, long_filter.reshape(1, count),
+        query_taps.T, key_taps.T, value_taps.T, *consts,
+    ]
     made = pl.pallas_call(
         kernel,
         out_shape=(token_out, token_out, token_out, filter_out),
         in_specs=[hbm] * (8 + len(consts)),
-        out_specs=(hbm, hbm, hbm, vmem),
+        out_specs=(vmem,) * 4,
         scratch_shapes=[pltpu.VMEM((channels, count), BF16)] * 4
         + [pltpu.VMEM((1, count), F32)]
         + [pltpu.SMEM((3, channels), F32)] * 3
@@ -330,39 +321,31 @@
             pltpu.VMEM((4 * channels, BLK), F32),
             pltpu.VMEM((NZ, 16, BLK), BF16),
             pltpu.VMEM((NZ, 16, BLK), BF16),
-            pltpu.VMEM((NZ, 1, BLK), F32),
+            pltpu.VMEM((NP, 1, BLK), F32),
             pltpu.VMEM((NI, 4, NZ, BLK), BF16),
             pltpu.VMEM((NP, 4, NZ, BLK), BF16),
-            pltpu.VMEM((NZ, BLK), F32),
-            pltpu.VMEM((NP, NZ, BLK), F32),
+            pltpu.VMEM((NZ, NP, 1, BLK), F32),
             pltpu.VMEM((5, NB, BLK), F32),
             pltpu.VMEM((2, NB, BLK), F32),
             pltpu.VMEM((NP, 2, NZ, BLK), F32),
             pltpu.VMEM((NP, 2, NZ, BLK), F32),
             pltpu.VMEM((NZ * 16, BLK), F32),
             pltpu.VMEM((NZ * 16, BLK), F32),
-            pltpu.VMEM((3, channels, BLK), F32),
             pltpu.VMEM((NZ, 1, BLK), F32),
-            pltpu.VMEM((NZ, 1, BLK), F32),
-            pltpu.VMEM((1, BLK), F32),
-            pltpu.VMEM((NG, 1, BLK), F32),
+            pltpu.VMEM((NZ * NG, 1, BLK), F32),
             sems((8 + len(consts),)),
         ]
-        + [sems(())] * 14
-        + [sems((3,)), sems(()), sems(())],
+        + [sems(())] * 14,
         compiler_params=pltpu.CompilerParams(
-            collective_id=0, has_side_effects=True, vmem_limit_bytes=56 * 1024 * 1024
+            collective_id=0, has_side_effects=True, vmem_limit_bytes=16 * 1024 * 1024
         ),
-    )(
-        query_branch, key_branch, value_branch, grad_out, long_filter.reshape(1, count),
-        query_taps.T, key_taps.T, value_taps.T, *consts,
-    )
+    )(*[pltpu.with_memory_space_constraint(arg, pltpu.HBM) for arg in args])
     outs = pl.pallas_call(
         passed,
         out_shape=(token_out, token_out, token_out, filter_out),
         in_specs=[vmem] * 4,
         out_specs=(vmem,) * 4,
-        compiler_params=pltpu.CompilerParams(vmem_limit_bytes=56 * 1024 * 1024),
+        compiler_params=pltpu.CompilerParams(vmem_limit_bytes=16 * 1024 * 1024),
     )(*made)
     return outs[0], outs[1], outs[2], outs[3].reshape(count)
 

time: 49.2 us -> 45.3 us (0.921)
  Pallas kernels: 48.3 us -> 44.5 us
    pallas_call x1, Pallas kernels: 46.8 us -> 43.8 us  [local(): pl.pallas_call(kernel, out_shape=(token_out, token_out, token_out, filter...]
    pallas_call x1, Pallas kernels: 1.44 us -> 0.65 us  [local(): pl.pallas_call(passed, out_shape=(token_out, token_out, token_out, filter...]
where the time goes in v5:
time: 45.3 us; the launch traced here: 45.1 us
  Pallas kernels  44.5 us (98%)
  between operations  0.64 us (1%)
    pallas_call x1, Pallas kernels, local(): pl.pallas_call(kernel, out_shape=(token_out, token_out, token_out, filter...  43.8 us

profile of v5, /device:TPU:1, one launch (start us, length us, event | category | flops | bytes accessed | tf_op | source)
XLA Modules:
  0.0 45.1 jit_solution(5113167274389307260)
XLA Ops:
  0.6 43.8 %shard_map.156 = (f32[64,128]{1,0:T(8,128)S(1)}, f32[64,128]{1,0:T(8,128)S(1)}, f32[64,128]{1,0:T(8,128)S(1)}, f32[1,128]{1,0:T(1,128)S(1)}) custom-call(bf16[64,128]{1,0:T(8,128)(2,1)} %q_hbm.1, bf16[64,128]{1,0:T(8,128)(2,1)} %k_hbm.1, bf16[64,128]{1,0:T(8,128)(2,1)} %v_hbm.1, bf16[64,128]{1,0:T(8,128)(2,1)} %g_hbm.1, f32[1,128]{1,0:T(1,128)} %bitcast.8, ...), custom_call_target="tpu_custom_call" | custom-call | tf_op jit(solution)/shard_map/pallas_call | solution.py:311
  44.4 0.6 %shard_map.157 = (f32[64,128]{1,0:T(8,128)}, f32[64,128]{1,0:T(8,128)}, f32[64,128]{1,0:T(8,128)}, f32[1,128]{1,0:T(1,128)}) custom-call(f32[64,128]{1,0:T(8,128)S(1)} %get-tuple-element.12.refs_0_, f32[64,128]{1,0:T(8,128)S(1)} %get-tuple-element.13.refs_1_, f32[64,128]{1,0:T(8,128)S(1)} %get-tuple-element.14.refs_2_, f32[1,128]{1,0:T(1,128)S(1)} %get-tuple-element.15.refs_3_), custom_call_target="tpu_custom_call" | custom-call | tf_op jit(solution)/shard_map/pallas_call | solution.py:343

commit v6 on v5

--- a/solution.py
+++ b/solution.py
@@ -18,7 +18,7 @@
 FULL = 2 * BLK * NB
 MESH = pl.DeviceIdType.MESH
 Z_STEPS = (8, 7, 9, 6, 10, 5, 11, 4, 12, 3, 13, 2, 14, 1, 15)
-ZG_STEPS = [(step, turn) for step in Z_STEPS + (0,) for turn in range(NG) if step or turn]
+QUARTER = NZ // NG
 F32, BF16 = jnp.float32, jnp.bfloat16
 
 
@@ -92,9 +92,9 @@
     oq_ref, ok_ref, ov_ref, of_ref,
     q_ref, k_ref, v_ref, g_ref, filt_ref, tq_ref, tk_ref, tv_ref,
     fo, tw, fi, ii, io,
-    stage, s1, r1, f1, s2, r2, f2, tok, res, s3, r3, s4, r4, s4f, r4f,
+    stage, s1, r1, f1, s2, r2, f2, tok, res, s3, r3, s3q, r3q, s4, r4, s4f, r4f,
     load_sem, z_send, z_recv, f1_send, f1_recv, p_send, p_recv, f2_send, f2_recv,
-    b_send, b_recv, c_send, c_recv, cf_send, cf_recv,
+    b_send, b_recv, q_send, q_recv, own_send, own_recv, c_send, c_recv, cf_send, cf_recv,
 ):
     me = lax.axis_index("ctx")
     grp = lax.axis_index("grp")
@@ -106,9 +106,8 @@
         other = (z + step) % NZ
         return other, {"ctx": (y * NZ + other) * NX + x}
 
-    def zg_peer(step, turn):
-        other, target = z_peer(step)
-        return other, {**target, "grp": (grp + turn) % NG}
+    def ctx_of(other_z, other_p):
+        return ((other_p // NX) * NZ + other_z) * NX + other_p % NX
 
     def p_peer(step):
         other = (p + step) % NP
@@ -127,8 +126,9 @@
     for load in loads[:5]:
         load.start()
     barrier = pltpu.get_barrier_semaphore()
-    targets = [zg_peer(step, turn)[1] for step, turn in ZG_STEPS]
+    targets = [z_peer(step)[1] for step in Z_STEPS]
     targets += [p_peer(step)[1] for step in range(1, NP)]
+    targets += [{"grp": (grp + turn) % NG} for turn in range(1, NG)]
     for target in targets:
         pl.semaphore_signal(barrier, inc=1, device_id=target, device_id_type=MESH)
 
@@ -256,34 +256,82 @@
     res[1] = jnp.where(first, cross_tok, back(main_tok * key_conv, taps[2]))
 
     for other in range(NP):
-        for n in range(2):
-            s3[other, n] = res[n, rows_of(other), :]
+        s3[other] = res[0, rows_of(other), :]
+        second = res[1, rows_of(other), :]
+        for part in range(NG):
+            s3q[other, part] = second[part * QUARTER : (part + 1) * QUARTER]
     for step in range(1, NP):
         other, target = p_peer(step)
         send(s3.at[other], r3.at[p], b_send, b_recv, target)
+        for part in range(NG):
+            member = role * grp + (1 - role) * part
+            slot = role * part + (1 - role) * grp
+            send(
+                s3q.at[other, part], r3q.at[p, slot], q_send, q_recv, {**target, "grp": member}
+            )
     r3[p] = s3[p]
+
+    @pl.when(role == 0)
+    def _():
+        for turn in range(1, NG):
+            part = (grp + turn) % NG
+            send(s3q.at[p, part], r3q.at[p, grp], own_send, own_recv, {"grp": part})
+        r3q[p, grp] = s3q[p, grp]
+        arrived(s3q.at[0, pl.ds(0, NG - 1)], own_send)
+        arrived(s3q.at[0, pl.ds(0, NG - 1)], own_recv)
+
+    @pl.when(role == 1)
+    def _():
+        r3q[p] = s3q[p]
+
+    arrived(r3q.at[pl.ds(0, NP - 1)], q_recv)
+
+    cross_rows = r3q[0, 0]
+    for i in range(NI):
+        for part in range(NG):
+            if i or part:
+                cross_rows = cross_rows + r3q[2 * i, part]
+            s4[pl.ds(2 * NI + i + part * QUARTER * 16, QUARTER, stride=16), :] = r3q[2 * i + 1, part]
+    s4f[...] = cross_rows.reshape(QUARTER, 1, BLK)
+    mine = z // QUARTER == grp
+    for row in range(QUARTER):
+        other = grp * QUARTER + row
+        for turn in range(1, NG):
+            target = {"ctx": ctx_of(other, p), "grp": (grp + turn) % NG}
+            send(s4f.at[row], r4f.at[z], cf_send, cf_recv, target)
+
+        @pl.when(other != z)
+        def _():
+            send(s4f.at[row], r4f.at[z], cf_send, cf_recv, {"ctx": ctx_of(other, p)})
+
+        @pl.when(other == z)
+        def _():
+            r4f[z] = s4f[row]
+
     arrived(r3.at[pl.ds(0, NP - 1)], b_recv)
-
-    s4f[...] = ((r3[0, 1] + r3[2, 1]) + (r3[4, 1] + r3[6, 1])).reshape(NZ, 1, BLK)
-    for step, turn in ZG_STEPS:
-        other, target = zg_peer(step, turn)
-        send(s4f.at[other], r4f.at[z * NG + grp], cf_send, cf_recv, target)
     for i in range(NI):
-        s4[pl.ds(i, NZ, stride=16), :] = r3[2 * i, 0]
-        s4[pl.ds(NI + i, NZ, stride=16), :] = r3[2 * i + 1, 0]
-        s4[pl.ds(2 * NI + i, NZ, stride=16), :] = r3[2 * i + 1, 1]
+        s4[pl.ds(i, NZ, stride=16), :] = r3[2 * i]
+        s4[pl.ds(NI + i, NZ, stride=16), :] = r3[2 * i + 1]
     my_rows = pl.ds(pl.multiple_of(z * 16, 16), 12)
     for step in Z_STEPS:
         other, target = z_peer(step)
         rows = pl.ds(pl.multiple_of(other * 16, 16), 12)
         send(s4.at[rows], r4.at[my_rows], c_send, c_recv, target)
     r4[my_rows, :] = s4[my_rows, :]
-    r4f[z * NG + grp] = s4f[z]
     arrived(r2.at[pl.ds(0, NP - 1)], p_send)
     arrived(r3.at[pl.ds(0, NP - 1)], b_send)
-    arrived(r4f.at[pl.ds(0, NZ * NG - 1)], cf_send)
-    arrived(r4f.at[pl.ds(0, NZ * NG - 1)], cf_recv)
-    of_ref[...] = jnp.sum(r4f[...].reshape(NZ * NG, BLK), axis=0, keepdims=True)
+    arrived(r3q.at[pl.ds(0, NP - 1)], q_send)
+    for sem in (cf_send, cf_recv):
+
+        @pl.when(mine)
+        def _():
+            arrived(r4f.at[pl.ds(0, NZ - 1)], sem)
+
+        @pl.when(jnp.logical_not(mine))
+        def _():
+            arrived(r4f, sem)
+
+    of_ref[...] = jnp.sum(r4f[...].reshape(NZ, BLK), axis=0, keepdims=True)
     arrived(r4.at[pl.ds(0, (NZ - 1) * 12)], c_recv)
     for n, ref in enumerate((oq_ref, ok_ref, ov_ref)):
         for i in range(NI):
@@ -327,15 +375,17 @@
             pltpu.VMEM((NZ, NP, 1, BLK), F32),
             pltpu.VMEM((5, NB, BLK), F32),
             pltpu.VMEM((2, NB, BLK), F32),
-            pltpu.VMEM((NP, 2, NZ, BLK), F32),
-            pltpu.VMEM((NP, 2, NZ, BLK), F32),
+            pltpu.VMEM((NP, NZ, BLK), F32),
+            pltpu.VMEM((NP, NZ, BLK), F32),
+            pltpu.VMEM((NP, NG, QUARTER, BLK), F32),
+            pltpu.VMEM((NP, NG, QUARTER, BLK), F32),
             pltpu.VMEM((NZ * 16, BLK), F32),
             pltpu.VMEM((NZ * 16, BLK), F32),
+            pltpu.VMEM((QUARTER, 1, BLK), F32),
             pltpu.VMEM((NZ, 1, BLK), F32),
-            pltpu.VMEM((NZ * NG, 1, BLK), F32),
             sems((8 + len(consts),)),
         ]
-        + [sems(())] * 14,
+        + [sems(())] * 18,
         compiler_params=pltpu.CompilerParams(
             collective_id=0, has_side_effects=True, vmem_limit_bytes=16 * 1024 * 1024
         ),

time: 45.3 us -> 45.5 us (level)
  no operation moved by 1% of the time
where the time goes in v6:
time: 45.5 us; the launch traced here: 45.3 us
  Pallas kernels  44.7 us (98%)
  between operations  0.64 us (1%)
    pallas_call x1, Pallas kernels, local(): pl.pallas_call(kernel, out_shape=(token_out, token_out, token_out, filter...  44 us

profile of v6, /device:TPU:1, one launch (start us, length us, event | category | flops | bytes accessed | tf_op | source)
XLA Modules:
  0.0 45.3 jit_solution(13096959153542050566)
XLA Ops:
  0.6 44.0 %shard_map.156 = (f32[64,128]{1,0:T(8,128)S(1)}, f32[64,128]{1,0:T(8,128)S(1)}, f32[64,128]{1,0:T(8,128)S(1)}, f32[1,128]{1,0:T(1,128)S(1)}) custom-call(bf16[64,128]{1,0:T(8,128)(2,1)} %q_hbm.1, bf16[64,128]{1,0:T(8,128)(2,1)} %k_hbm.1, bf16[64,128]{1,0:T(8,128)(2,1)} %v_hbm.1, bf16[64,128]{1,0:T(8,128)(2,1)} %g_hbm.1, f32[1,128]{1,0:T(1,128)} %bitcast.8, ...), custom_call_target="tpu_custom_call" | custom-call | tf_op jit(solution)/shard_map/pallas_call | solution.py:359
  44.7 0.6 %shard_map.157 = (f32[64,128]{1,0:T(8,128)}, f32[64,128]{1,0:T(8,128)}, f32[64,128]{1,0:T(8,128)}, f32[1,128]{1,0:T(1,128)}) custom-call(f32[64,128]{1,0:T(8,128)S(1)} %get-tuple-element.12.refs_0_, f32[64,128]{1,0:T(8,128)S(1)} %get-tuple-element.13.refs_1_, f32[64,128]{1,0:T(8,128)S(1)} %get-tuple-element.14.refs_2_, f32[1,128]{1,0:T(1,128)S(1)} %get-tuple-element.15.refs_3_), custom_call_target="tpu_custom_call" | custom-call | tf_op jit(solution)/shard_map/pallas_call | solution.py:393

commit v7 on v5

--- a/solution.py
+++ b/solution.py
@@ -124,15 +124,14 @@
             )
         )
     ]
-    for load in loads[:5]:
-        load.start()
     barrier = pltpu.get_barrier_semaphore()
-    targets = [zg_peer(step, turn)[1] for step, turn in ZG_STEPS]
+    targets = [z_peer(step)[1] for step in Z_STEPS]
     targets += [p_peer(step)[1] for step in range(1, NP)]
+    targets += [{"grp": (grp + turn) % NG} for turn in range(1, NG)]
     for target in targets:
         pl.semaphore_signal(barrier, inc=1, device_id=target, device_id_type=MESH)
 
-    for load in loads[5:]:
+    for load in loads:
         load.start()
 
     def send(src, dst, send_sem, recv_sem, target):
@@ -155,13 +154,13 @@
     f1[p] = filt_ref[...]
     pl.semaphore_wait(barrier, len(targets))
 
-    for step in range(1, NP):
-        send(filt_ref, f1.at[p], f1_send, f1_recv, p_peer(step)[1])
-
     for step in Z_STEPS:
         other, target = z_peer(step)
         send(s1.at[other], r1.at[z], z_send, z_recv, target)
     r1[z] = s1[z]
+
+    for step in range(1, NP):
+        send(filt_ref, f1.at[p], f1_send, f1_recv, p_peer(step)[1])
     arrived(f1.at[pl.ds(0, NP - 1)], f1_recv)
     for step in Z_STEPS:
         send(f1, f2.at[z], f2_send, f2_recv, z_peer(step)[1])
@@ -265,18 +264,20 @@
     arrived(r3.at[pl.ds(0, NP - 1)], b_recv)
 
     s4f[...] = ((r3[0, 1] + r3[2, 1]) + (r3[4, 1] + r3[6, 1])).reshape(NZ, 1, BLK)
-    for step, turn in ZG_STEPS:
-        other, target = zg_peer(step, turn)
-        send(s4f.at[other], r4f.at[z * NG + grp], cf_send, cf_recv, target)
     for i in range(NI):
         s4[pl.ds(i, NZ, stride=16), :] = r3[2 * i, 0]
         s4[pl.ds(NI + i, NZ, stride=16), :] = r3[2 * i + 1, 0]
         s4[pl.ds(2 * NI + i, NZ, stride=16), :] = r3[2 * i + 1, 1]
     my_rows = pl.ds(pl.multiple_of(z * 16, 16), 12)
-    for step in Z_STEPS:
-        other, target = z_peer(step)
-        rows = pl.ds(pl.multiple_of(other * 16, 16), 12)
-        send(s4.at[rows], r4.at[my_rows], c_send, c_recv, target)
+    for step in Z_STEPS + (0,):
+        for turn in range(NG):
+            other, target = zg_peer(step, turn)
+            if step or turn:
+                send(s4f.at[other], r4f.at[z * NG + grp], cf_send, cf_recv, target)
+        if step:
+            other, target = z_peer(step)
+            rows = pl.ds(pl.multiple_of(other * 16, 16), 12)
+            send(s4.at[rows], r4.at[my_rows], c_send, c_recv, target)
     r4[my_rows, :] = s4[my_rows, :]
     r4f[z * NG + grp] = s4f[z]
     arrived(r2.at[pl.ds(0, NP - 1)], p_send)

time: 45.3 us -> 44.8 us (0.989)
  Pallas kernels: 44.5 us -> 44 us
    pallas_call x1, Pallas kernels: 43.8 us -> 43.3 us  [local(): pl.pallas_call(kernel, out_shape=(token_out, token_out, token_out, filter...]
where the time goes in v7:
time: 44.8 us; the launch traced here: 44.6 us
  Pallas kernels  44 us (98%)
  between operations  0.64 us (1%)
    pallas_call x1, Pallas kernels, local(): pl.pallas_call(kernel, out_shape=(token_out, token_out, token_out, filter...  43.3 us

profile of v7, /device:TPU:1, one launch (start us, length us, event | category | flops | bytes accessed | tf_op | source)
XLA Modules:
  0.0 44.6 jit_solution(3203943498569211717)
XLA Ops:
  0.6 43.3 %shard_map.156 = (f32[64,128]{1,0:T(8,128)S(1)}, f32[64,128]{1,0:T(8,128)S(1)}, f32[64,128]{1,0:T(8,128)S(1)}, f32[1,128]{1,0:T(1,128)S(1)}) custom-call(bf16[64,128]{1,0:T(8,128)(2,1)} %q_hbm.1, bf16[64,128]{1,0:T(8,128)(2,1)} %k_hbm.1, bf16[64,128]{1,0:T(8,128)(2,1)} %v_hbm.1, bf16[64,128]{1,0:T(8,128)(2,1)} %g_hbm.1, f32[1,128]{1,0:T(1,128)} %bitcast.8, ...), custom_call_target="tpu_custom_call" | custom-call | tf_op jit(solution)/shard_map/pallas_call | solution.py:312
  44.0 0.6 %shard_map.157 = (f32[64,128]{1,0:T(8,128)}, f32[64,128]{1,0:T(8,128)}, f32[64,128]{1,0:T(8,128)}, f32[1,128]{1,0:T(1,128)}) custom-call(f32[64,128]{1,0:T(8,128)S(1)} %get-tuple-element.12.refs_0_, f32[64,128]{1,0:T(8,128)S(1)} %get-tuple-element.13.refs_1_, f32[64,128]{1,0:T(8,128)S(1)} %get-tuple-element.14.refs_2_, f32[1,128]{1,0:T(1,128)S(1)} %get-tuple-element.15.refs_3_), custom_call_target="tpu_custom_call" | custom-call | tf_op jit(solution)/shard_map/pallas_call | solution.py:344

commit v8 on v7

--- a/solution.py
+++ b/solution.py
@@ -94,7 +94,7 @@
     fo, tw, fi, ii, io,
     stage, s1, r1, f1, s2, r2, f2, tok, res, s3, r3, s4, r4, s4f, r4f,
     load_sem, z_send, z_recv, f1_send, f1_recv, p_send, p_recv, f2_send, f2_recv,
-    b_send, b_recv, c_send, c_recv, cf_send, cf_recv,
+    b_send, b_recv, d_send, d_recv, c_send, c_recv, cf_send, cf_recv,
 ):
     me = lax.axis_index("ctx")
     grp = lax.axis_index("grp")
@@ -256,32 +256,37 @@
 
     for other in range(NP):
         for n in range(2):
-            s3[other, n] = res[n, rows_of(other), :]
+            s3[n, other] = res[n, rows_of(other), :]
     for step in range(1, NP):
         other, target = p_peer(step)
-        send(s3.at[other], r3.at[p], b_send, b_recv, target)
-    r3[p] = s3[p]
-    arrived(r3.at[pl.ds(0, NP - 1)], b_recv)
-
-    s4f[...] = ((r3[0, 1] + r3[2, 1]) + (r3[4, 1] + r3[6, 1])).reshape(NZ, 1, BLK)
+        send(s3.at[1, other], r3.at[1, p], d_send, d_recv, target)
+    for step in range(1, NP):
+        other, target = p_peer(step)
+        send(s3.at[0, other], r3.at[0, p], b_send, b_recv, target)
+    for n in range(2):
+        r3[n, p] = s3[n, p]
+    arrived(r3.at[1, pl.ds(0, NP - 1)], d_recv)
+
+    s4f[...] = ((r3[1, 0] + r3[1, 2]) + (r3[1, 4] + r3[1, 6])).reshape(NZ, 1, BLK)
+    for step in Z_STEPS + (0,):
+        for turn in range(1 if step == 0 else 0, NG):
+            other, target = zg_peer(step, turn)
+            send(s4f.at[other], r4f.at[z * NG + grp], cf_send, cf_recv, target)
+    arrived(r3.at[0, pl.ds(0, NP - 1)], b_recv)
     for i in range(NI):
-        s4[pl.ds(i, NZ, stride=16), :] = r3[2 * i, 0]
-        s4[pl.ds(NI + i, NZ, stride=16), :] = r3[2 * i + 1, 0]
-        s4[pl.ds(2 * NI + i, NZ, stride=16), :] = r3[2 * i + 1, 1]
+        s4[pl.ds(i, NZ, stride=16), :] = r3[0, 2 * i]
+        s4[pl.ds(NI + i, NZ, stride=16), :] = r3[0, 2 * i + 1]
+        s4[pl.ds(2 * NI + i, NZ, stride=16), :] = r3[1, 2 * i + 1]
     my_rows = pl.ds(pl.multiple_of(z * 16, 16), 12)
-    for step in Z_STEPS + (0,):
-        for turn in range(NG):
-            other, target = zg_peer(step, turn)
-            if step or turn:
-                send(s4f.at[other], r4f.at[z * NG + grp], cf_send, cf_recv, target)
-        if step:
-            other, target = z_peer(step)
-            rows = pl.ds(pl.multiple_of(other * 16, 16), 12)
-            send(s4.at[rows], r4.at[my_rows], c_send, c_recv, target)
+    for step in Z_STEPS:
+        other, target = z_peer(step)
+        rows = pl.ds(pl.multiple_of(other * 16, 16), 12)
+        send(s4.at[rows], r4.at[my_rows], c_send, c_recv, target)
     r4[my_rows, :] = s4[my_rows, :]
     r4f[z * NG + grp] = s4f[z]
     arrived(r2.at[pl.ds(0, NP - 1)], p_send)
-    arrived(r3.at[pl.ds(0, NP - 1)], b_send)
+    arrived(r3.at[0, pl.ds(0, NP - 1)], b_send)
+    arrived(r3.at[0, pl.ds(0, NP - 1)], d_send)
     arrived(r4f.at[pl.ds(0, NZ * NG - 1)], cf_send)
     arrived(r4f.at[pl.ds(0, NZ * NG - 1)], cf_recv)
     of_ref[...] = jnp.sum(r4f[...].reshape(NZ * NG, BLK), axis=0, keepdims=True)
@@ -328,15 +333,15 @@
             pltpu.VMEM((NZ, NP, 1, BLK), F32),
             pltpu.VMEM((5, NB, BLK), F32),
             pltpu.VMEM((2, NB, BLK), F32),
-            pltpu.VMEM((NP, 2, NZ, BLK), F32),
-            pltpu.VMEM((NP, 2, NZ, BLK), F32),
+            pltpu.VMEM((2, NP, NZ, BLK), F32),
+            pltpu.VMEM((2, NP, NZ, BLK), F32),
             pltpu.VMEM((NZ * 16, BLK), F32),
             pltpu.VMEM((NZ * 16, BLK), F32),
             pltpu.VMEM((NZ, 1, BLK), F32),
             pltpu.VMEM((NZ * NG, 1, BLK), F32),
             sems((8 + len(consts),)),
         ]
-        + [sems(())] * 14,
+        + [sems(())] * 16,
         compiler_params=pltpu.CompilerParams(
             collective_id=0, has_side_effects=True, vmem_limit_bytes=16 * 1024 * 1024
         ),

time: 44.8 us -> 44.6 us (level)
  no operation moved by 1% of the time
where the time goes in v8:
time: 44.6 us; the launch traced here: 44.4 us
  Pallas kernels  43.7 us (98%)
  between operations  0.64 us (1%)
    pallas_call x1, Pallas kernels, local(): pl.pallas_call(kernel, out_shape=(token_out, token_out, token_out, filter...  43.1 us

profile of v8, /device:TPU:1, one launch (start us, length us, event | category | flops | bytes accessed | tf_op | source)
XLA Modules:
  0.0 44.4 jit_solution(9271304529970248229)
XLA Ops:
  0.6 43.1 %shard_map.156 = (f32[64,128]{1,0:T(8,128)S(1)}, f32[64,128]{1,0:T(8,128)S(1)}, f32[64,128]{1,0:T(8,128)S(1)}, f32[1,128]{1,0:T(1,128)S(1)}) custom-call(bf16[64,128]{1,0:T(8,128)(2,1)} %q_hbm.1, bf16[64,128]{1,0:T(8,128)(2,1)} %k_hbm.1, bf16[64,128]{1,0:T(8,128)(2,1)} %v_hbm.1, bf16[64,128]{1,0:T(8,128)(2,1)} %g_hbm.1, f32[1,128]{1,0:T(1,128)} %bitcast.8, ...), custom_call_target="tpu_custom_call" | custom-call | tf_op jit(solution)/shard_map/pallas_call | solution.py:317
  43.7 0.6 %shard_map.157 = (f32[64,128]{1,0:T(8,128)}, f32[64,128]{1,0:T(8,128)}, f32[64,128]{1,0:T(8,128)}, f32[1,128]{1,0:T(1,128)}) custom-call(f32[64,128]{1,0:T(8,128)S(1)} %get-tuple-element.12.refs_0_, f32[64,128]{1,0:T(8,128)S(1)} %get-tuple-element.13.refs_1_, f32[64,128]{1,0:T(8,128)S(1)} %get-tuple-element.14.refs_2_, f32[1,128]{1,0:T(1,128)S(1)} %get-tuple-element.15.refs_3_), custom_call_target="tpu_custom_call" | custom-call | tf_op jit(solution)/shard_map/pallas_call | solution.py:349

commit v9 on v8

--- a/solution.py
+++ b/solution.py
@@ -154,13 +154,13 @@
     f1[p] = filt_ref[...]
     pl.semaphore_wait(barrier, len(targets))
 
+    for step in range(1, NP):
+        send(filt_ref, f1.at[p], f1_send, f1_recv, p_peer(step)[1])
+
     for step in Z_STEPS:
         other, target = z_peer(step)
         send(s1.at[other], r1.at[z], z_send, z_recv, target)
     r1[z] = s1[z]
-
-    for step in range(1, NP):
-        send(filt_ref, f1.at[p], f1_send, f1_recv, p_peer(step)[1])
     arrived(f1.at[pl.ds(0, NP - 1)], f1_recv)
     for step in Z_STEPS:
         send(f1, f2.at[z], f2_send, f2_recv, z_peer(step)[1])

time: 44.6 us -> 44.6 us (level)
  no operation moved by 1% of the time
where the time goes in v9:
time: 44.6 us; the launch traced here: 44.4 us
  Pallas kernels  43.7 us (98%)
  between operations  0.64 us (1%)
    pallas_call x1, Pallas kernels, local(): pl.pallas_call(kernel, out_shape=(token_out, token_out, token_out, filter...  43.1 us

profile of v9, /device:TPU:1, one launch (start us, length us, event | category | flops | bytes accessed | tf_op | source)
XLA Modules:
  0.0 44.4 jit_solution(3430396784547285120)
XLA Ops:
  0.6 43.1 %shard_map.156 = (f32[64,128]{1,0:T(8,128)S(1)}, f32[64,128]{1,0:T(8,128)S(1)}, f32[64,128]{1,0:T(8,128)S(1)}, f32[1,128]{1,0:T(1,128)S(1)}) custom-call(bf16[64,128]{1,0:T(8,128)(2,1)} %q_hbm.1, bf16[64,128]{1,0:T(8,128)(2,1)} %k_hbm.1, bf16[64,128]{1,0:T(8,128)(2,1)} %v_hbm.1, bf16[64,128]{1,0:T(8,128)(2,1)} %g_hbm.1, f32[1,128]{1,0:T(1,128)} %bitcast.8, ...), custom_call_target="tpu_custom_call" | custom-call | tf_op jit(solution)/shard_map/pallas_call | solution.py:317
  43.7 0.6 %shard_map.157 = (f32[64,128]{1,0:T(8,128)}, f32[64,128]{1,0:T(8,128)}, f32[64,128]{1,0:T(8,128)}, f32[1,128]{1,0:T(1,128)}) custom-call(f32[64,128]{1,0:T(8,128)S(1)} %get-tuple-element.12.refs_0_, f32[64,128]{1,0:T(8,128)S(1)} %get-tuple-element.13.refs_1_, f32[64,128]{1,0:T(8,128)S(1)} %get-tuple-element.14.refs_2_, f32[1,128]{1,0:T(1,128)S(1)} %get-tuple-element.15.refs_3_), custom_call_target="tpu_custom_call" | custom-call | tf_op jit(solution)/shard_map/pallas_call | solution.py:349

commit v10 on v9

--- a/solution.py
+++ b/solution.py
@@ -17,6 +17,7 @@
 NB = NY * NZ * NX
 FULL = 2 * BLK * NB
 MESH = pl.DeviceIdType.MESH
+P_STEPS = ((1, 2), (1, 1), (1, 3), (1, 0), (0, 2), (0, 1), (0, 3))
 Z_STEPS = (8, 7, 9, 6, 10, 5, 11, 4, 12, 3, 13, 2, 14, 1, 15)
 ZG_STEPS = [(step, turn) for step in Z_STEPS + (0,) for turn in range(NG) if step or turn]
 F32, BF16 = jnp.float32, jnp.bfloat16
@@ -111,7 +112,8 @@
         return other, {**target, "grp": (grp + turn) % NG}
 
     def p_peer(step):
-        other = (p + step) % NP
+        up, along = P_STEPS[step - 1]
+        other = ((y + up) % NY) * NX + (x + along) % NX
         return other, {"ctx": ((other // NX) * NZ + z) * NX + other % NX}
 
     loads = [

time: 44.6 us -> 44.5 us (level)
  no operation moved by 1% of the time
where the time goes in v10:
time: 44.5 us; the launch traced here: 44.3 us
  Pallas kernels  43.7 us (98%)
  between operations  0.64 us (1%)
    pallas_call x1, Pallas kernels, local(): pl.pallas_call(kernel, out_shape=(token_out, token_out, token_out, filter...  43 us

profile of v10, /device:TPU:1, one launch (start us, length us, event | category | flops | bytes accessed | tf_op | source)
XLA Modules:
  0.0 44.3 jit_solution(2593686333075265454)
XLA Ops:
  0.6 43.0 %shard_map.156 = (f32[64,128]{1,0:T(8,128)S(1)}, f32[64,128]{1,0:T(8,128)S(1)}, f32[64,128]{1,0:T(8,128)S(1)}, f32[1,128]{1,0:T(1,128)S(1)}) custom-call(bf16[64,128]{1,0:T(8,128)(2,1)} %q_hbm.1, bf16[64,128]{1,0:T(8,128)(2,1)} %k_hbm.1, bf16[64,128]{1,0:T(8,128)(2,1)} %v_hbm.1, bf16[64,128]{1,0:T(8,128)(2,1)} %g_hbm.1, f32[1,128]{1,0:T(1,128)} %bitcast.8, ...), custom_call_target="tpu_custom_call" | custom-call | tf_op jit(solution)/shard_map/pallas_call | solution.py:319
  43.7 0.6 %shard_map.157 = (f32[64,128]{1,0:T(8,128)}, f32[64,128]{1,0:T(8,128)}, f32[64,128]{1,0:T(8,128)}, f32[1,128]{1,0:T(1,128)}) custom-call(f32[64,128]{1,0:T(8,128)S(1)} %get-tuple-element.12.refs_0_, f32[64,128]{1,0:T(8,128)S(1)} %get-tuple-element.13.refs_1_, f32[64,128]{1,0:T(8,128)S(1)} %get-tuple-element.14.refs_2_, f32[1,128]{1,0:T(1,128)S(1)} %get-tuple-element.15.refs_3_), custom_call_target="tpu_custom_call" | custom-call | tf_op jit(solution)/shard_map/pallas_call | solution.py:351
